TPU v7x, 256 devices: a whole 4x4x8 slice. The times are simulated.
256 devices in a mesh: band: 4 (over z_hi, core), sx: 4 (over x), sy: 16 (over y, z_lo).
Axes of the slice: x: 4, y: 4, z: 8 (z_hi: 2, z_lo: 4; z = z_hi * 4 + z_lo), core: 2. Of those that a mesh axis runs over, the one named last changes fastest.
Arguments:
- orbitals: float32 [256, 24, 96, 128], P('band', 'sx', 'sy'), may hold values from -6 to 6
- potential: float32 [24, 96, 128], P('sx', 'sy'), may hold values from -3 to 0
- projectors: float32 [256, 4, 5, 128], P(('sx', 'sy')), may hold values from -0.25 to 0.25
- energies: float32 [256, 4], P(('sx', 'sy')), may hold values from 1 to 6
- centers: int32 [256, 2], P(('sx', 'sy')), may hold values from 0 to 95, as said below
Outputs:
- filtered: float32 [256, 24, 96, 128], P('band', 'sx', 'sy')
- gram: float32 [256, 256], P('band')
Inputs may be any that keep to these rules, and one draw needn't show every extreme that they name: `centers`: atom a's cell lies in the grid slab of the device numbered a // 4 along sx+sy, sy counting fastest; the first entry indexes the first grid dimension, the second the second.
All inputs are finite; a program needn't handle non-finite values.
Results may differ from a plain program's by a relative error of at most 0.0022.
Values may be sent and summed in bfloat16 or wider, within the bound.
A program may use at most 64 MiB of HBM per device.

v0:
```python
import jax
import jax.numpy as jnp
from jax import lax
from jax.sharding import PartitionSpec as P

stencil_weights = (
    -5369.0 / 1800.0,
    12.0 / 7.0,
    -15.0 / 56.0,
    10.0 / 189.0,
    -1.0 / 112.0,
    2.0 / 1925.0,
    -1.0 / 16632.0,
)
filter_center = 6.5
filter_half = 6.0
offsets_x = (0, -1, 1, 0, 0)
offsets_y = (0, 0, 0, -1, 1)


def from_behind(block, axis, distance):
    devices = range(lax.axis_size(axis))
    route = [(i - distance, i) for i in devices if i - distance in devices]
    return lax.ppermute(block, axis, route)


def extended(cells, sides, width):
    for axis, dim in sides:
        count = lax.axis_size(axis)
        ends = count - 1
        head = lax.slice_in_dim(cells, 0, width, axis=dim)
        tail = lax.slice_in_dim(cells, cells.shape[dim] - width, cells.shape[dim], axis=dim)
        cells = jnp.concatenate(
            [
                lax.ppermute(tail, axis, [(i, (i + 1) % count) for i in range(ends)]),
                cells,
                lax.ppermute(head, axis, [((i + 1) % count, i) for i in range(ends)]),
            ],
            axis=dim,
        )
    return cells


def second_sum(ext_x, ext_y, field):
    count_x = field.shape[1]
    count_y = field.shape[2]
    count_z = field.shape[3]
    padded_z = jnp.pad(field, ((0, 0), (0, 0), (0, 0), (6, 6)))
    total = 3.0 * stencil_weights[0] * field
    for step in range(1, 7):
        weight = stencil_weights[step]
        total = total + weight * (
            ext_x[:, 6 + step : 6 + step + count_x] + ext_x[:, 6 - step : 6 - step + count_x]
        )
        total = total + weight * (
            ext_y[:, :, 6 + step : 6 + step + count_y] + ext_y[:, :, 6 - step : 6 - step + count_y]
        )
        total = total + weight * (
            padded_z[:, :, :, 6 + step : 6 + step + count_z]
            + padded_z[:, :, :, 6 - step : 6 - step + count_z]
        )
    return total


def column_slots(centers, first_x, first_y, count_x, count_y):
    shift_x = jnp.array(offsets_x, jnp.int32)
    shift_y = jnp.array(offsets_y, jnp.int32)
    local_x = centers[:, 0:1] - first_x + shift_x[None, :]
    local_y = centers[:, 1:2] - first_y + shift_y[None, :]
    inner = count_x * count_y
    slots = jnp.where(
        local_x < 0,
        inner + local_y,
        jnp.where(
            local_x >= count_x,
            inner + count_y + local_y,
            jnp.where(
                local_y < 0,
                inner + 2 * count_y + local_x,
                jnp.where(
                    local_y >= count_y,
                    inner + 2 * count_y + count_x + local_x,
                    local_x * count_y + local_y,
                ),
            ),
        ),
    )
    return slots.reshape(-1)


def pass_x(strip, offset):
    return from_behind(strip.astype(jnp.bfloat16), "sx", offset).astype(strip.dtype)


def pass_y(strip, offset):
    return from_behind(strip, "sy", offset)


def nonlocal_term(field, ext_x, ext_y, slots, projectors, energies):
    batch, count_x, count_y, count_z = field.shape
    inner = count_x * count_y
    tiles = projectors.shape[2]
    atoms = projectors.shape[0]
    table = jnp.concatenate(
        [
            field.reshape(batch, inner, count_z),
            ext_x[:, 5],
            ext_x[:, 6 + count_x],
            ext_y[:, :, 5],
            ext_y[:, :, 6 + count_y],
        ],
        axis=1,
    )
    onehot = (slots[:, None] == jnp.arange(table.shape[1], dtype=jnp.int32)[None, :]).astype(
        jnp.float32
    )
    picked = jnp.einsum("kc,bcz->bkz", onehot, table, precision=lax.Precision.HIGHEST).reshape(
        batch, atoms, tiles, count_z
    )
    coeffs = jnp.einsum("aptz,batz->bap", projectors, picked, precision=lax.Precision.HIGHEST)
    weighted = coeffs * energies[None]
    spread = jnp.einsum(
        "aptz,bap->batz", projectors, weighted, precision=lax.Precision.HIGHEST
    ).reshape(batch, atoms * tiles, count_z)
    back = jnp.einsum("kc,bkz->bcz", onehot, spread, precision=lax.Precision.HIGHEST)
    result = back[:, :inner].reshape(batch, count_x, count_y, count_z)
    from_right = pass_x(back[:, inner : inner + count_y], -1)
    from_left = pass_x(back[:, inner + count_y : inner + 2 * count_y], 1)
    result = result.at[:, count_x - 1].add(from_right)
    result = result.at[:, 0].add(from_left)
    base_y = inner + 2 * count_y
    from_above = pass_y(back[:, base_y : base_y + count_x], -1)
    from_below = pass_y(back[:, base_y + count_x : base_y + 2 * count_x], 1)
    result = result.at[:, :, count_y - 1].add(from_above)
    result = result.at[:, :, 0].add(from_below)
    return result


def local(orbitals, potential, projectors, energies, centers):
    first_y = lax.axis_index("sy") * potential.shape[1]
    pot_all, proj_all, energy_all = (potential, projectors, energies)
    slots = column_slots(
        centers,
        lax.axis_index("sx") * potential.shape[0],
        first_y,
        orbitals.shape[1],
        orbitals.shape[2],
    )

    def apply_h(vector):
        ext_x = extended(vector, (("sx", 1),), 6)
        ext_y = extended(vector, (("sy", 2),), 6)
        kinetic = -0.5 * second_sum(ext_x, ext_y, vector)
        return (
            kinetic
            + pot_all[None] * vector
            + nonlocal_term(vector, ext_x, ext_y, slots, proj_all, energy_all)
        )

    previous = orbitals
    current = (apply_h(orbitals) - filter_center * orbitals) / filter_half
    following = 2.0 * (apply_h(current) - filter_center * current) / filter_half - previous
    previous, current = (current, following)
    rounded = current.astype(jnp.bfloat16)
    flat = rounded.reshape(rounded.shape[0], -1)
    partial_rows = lax.dot_general(
        flat,
        lax.all_gather(flat, "band", axis=0, tiled=True),
        (((1,), (1,)), ((), ())),
        preferred_element_type=jnp.float32,
    )
    cell_total = flat.shape[1] * lax.axis_size("sx") * lax.axis_size("sy")
    gram = lax.psum(partial_rows, ("sx", "sy")) / cell_total
    return (current, gram)


def solution(mesh):
    in_specs = (
        P("band", "sx", "sy", None),
        P("sx", "sy", None),
        P(("sx", "sy"), None, None, None),
        P(("sx", "sy"), None),
        P(("sx", "sy"), None),
    )
    out_specs = (P("band", "sx", "sy", None), P("band", None))
    return jax.shard_map(local, mesh=mesh, in_specs=in_specs, out_specs=out_specs, check_vma=False)
```

profile of v0, /device:TPU:1, one launch (start us, length us, event | category | flops | bytes accessed | tf_op | source)
XLA Modules:
  0.0 941.9 jit_solution(861587233101737842)
XLA Ops:
  7.3 1.3 collective-permute-start
  8.6 4.7 collective-permute-start.1
  13.2 4.9 collective-permute-start.3
  18.1 1.3 collective-permute-start.2
  19.4 3.1 copy.96
  22.7 12.1 %collective-permute-done = f32[64,6,6,128]{3,0,2,1:T(8,128)S(1)} collective-permute-done((f32[64,6,6,128]{3,0,2,1:T(8,128)}, f32[64,6,6,128]{3,0,2,1:T(8,128)S(1)}, u32[]{:S(2)}, u32[]{:S(2)}) %collective-permute-start) | collective-permute-done | bytes 1179680 | tf_op jit(solution)/shard_map/ppermute | solution.py:37
  34.9 0.9 collective-permute-done.1
  35.8 1.0 copy.168
  36.9 4.5 collective-permute-done.3
  41.3 2.0 copy_dynamic-update-slice_fusion.2
  43.3 2.5 copy_dynamic-update-slice_fusion
  45.8 25.9 %collective-permute-done.2 = f32[64,6,6,128]{3,0,2,1:T(8,128)} collective-permute-done((f32[64,6,6,128]{3,0,2,1:T(8,128)}, f32[64,6,6,128]{3,0,2,1:T(8,128)}, u32[]{:S(2)}, u32[]{:S(2)}) %collective-permute-start.2) | collective-permute-done | bytes 1179680 | tf_op jit(solution)/shard_map/ppermute | solution.py:37
  71.7 3.1 copy_dynamic-update-slice_fusion.3
  74.8 0.9 slice_bitcast_fusion.2
  75.7 14.2 %concatenate.86 = f32[64,60,128]{2,1,0:T(8,128)} concatenate(f32[64,36,128]{2,1,0:T(8,128)} %copy.96, f32[64,6,128]{2,1,0:T(8,128)} %bitcast.115, f32[64,6,128]{2,1,0:T(8,128)S(1)} %bitcast.114, f32[64,6,128]{2,1,0:T(8,128)} %get-tuple-element.126, f32[64,6,128]{2,1,0:T(8,128)} %get-tuple-element.125), dimensions={1} | concatenate | bytes 3932160 | tf_op jit(solution)/shard_map/concatenate | solution.py:104
  89.8 2.5 convolution_bitcast_fusion.3
  92.5 0.7 fusion.130
  93.2 0.8 fusion.158
  94.1 1.4 convolution_bitcast_fusion.1
  95.5 1.1 copy.158
  96.6 1.3 collective-permute-start.4
  97.9 0.9 fusion.155
  99.2 4.1 collective-permute-start.5
  103.3 1.3 collective-permute-start.6
  104.6 4.7 collective-permute-start.7
  109.3 1.9 copy.78
  111.2 1.8 copy.79
  113.1 1.8 copy.102
  115.2 6.1 scatter-add.29
  121.2 1.8 fusion.136
  123.0 1.8 fusion.135
  124.8 34.7 %broadcast_multiply_fusion = (f32[64,6,6,128]{3,1,0,2:T(8,128)S(1)}, f32[64,6,6,128]{3,1,0,2:T(8,128)}) fusion(f32[64,6,6,128]{3,1,0,2:T(8,128)} %get-tuple-element.116, f32[64,6,6,128]{3,1,0,2:T(8,128)} %fusion.135, f32[6,6,128]{2,0,1:T(8,128)S(1)} %copy.90, f32[64,6,6,128]{3,0,2,1:T(8,128)} %collective-permute-done.3, ...), kind=kLoop, calls=%fused_computation.225 | loop fusion | flops 21233664 | bytes 21252096 | tf_op jit(solution)/shard_map/div | solution.py:161
  159.7 1.3 collective-permute-start.8
  161.0 1.3 collective-permute-start.10
  162.3 4.1 collective-permute-start.11
  166.4 4.3 collective-permute-start.9
  171.4 16.0 %collective-permute-done.8 = f32[64,6,6,128]{3,0,2,1:T(8,128)S(1)} collective-permute-done((f32[64,6,6,128]{3,0,2,1:T(8,128)S(1)}, f32[64,6,6,128]{3,0,2,1:T(8,128)S(1)}, u32[]{:S(2)}, u32[]{:S(2)}) %collective-permute-start.8) | collective-permute-done | bytes 1179680 | tf_op jit(solution)/shard_map/ppermute | solution.py:37
  187.4 1.1 copy.165
  190.5 0.8 slice_bitcast_fusion
  192.0 1.2 collective-permute-done.9
  193.2 1.0 copy.166
  194.3 6.5 concatenate.91
  200.8 0.9 convolution_bitcast_fusion.2
  202.6 0.8 fusion.159
  203.5 1.4 convolution_bitcast_fusion
  204.9 1.1 copy.157
  206.0 1.3 collective-permute-start.12
  207.3 0.8 fusion.154
  208.6 4.9 collective-permute-start.13
  213.4 1.3 collective-permute-start.14
  214.7 4.3 collective-permute-start.15
  219.0 1.9 copy.105
  220.9 1.9 copy.107
  222.9 1.8 copy.128
  225.0 6.2 scatter-add.35
  231.2 1.7 fusion.134
  232.9 1.7 fusion.133
  234.6 15.2 %fusion.152 = (bf16[64,6,6,128]{3,1,0,2:T(8,128)(2,1)S(1)}, f32[64,6,6,128]{3,1,0,2:T(8,128)}) fusion(f32[64,6,6,128]{3,0,2,1:T(8,128)S(1)} %copy-done.4, f32[64,6,6,128]{3,1,0,2:T(8,128)} %get-tuple-element.107, f32[64,6,6,128]{3,1,0,2:T(8,128)} %fusion.133, f32[6,6,128]{2,0,1:T(8,128)S(1)} %copy.116, f32[64,6,6,128]{3,1,0,2:T(8,128)} %copy-done.5, ...), kind=kLoop, calls=%fused_computation.274 | loop fusion | flops 24772608 | bytes 11225088 | tf_op jit(solution)/shard_map/convert_element_type | solution.py:164
  250.5 1.5 reshape.394
  252.0 78.4 %all-gather.2.cloned.1.call-done = bf16[256,4608]{1,0:T(8,128)(2,1)} async-done(((bf16[64,4608]{1,0:T(8,128)(2,1)}), bf16[256,4608]{1,0:T(8,128)(2,1)}) %all-gather.2.cloned.1.call-update) | async-done | bytes 2359312 | tf_op jit(solution)/shard_map/all_gather | solution.py:168
  330.4 3.3 fusion.160
  333.7 1.2 copy.131
  334.9 598.7 %all-reduce.4.cloned.1.call-done = f32[64,256]{1,0:T(8,128)} async-done(((f32[64,256]{1,0:T(8,128)}), f32[64,256]{1,0:T(8,128)}) %all-reduce.4.cloned.1.call-update) | async-done | bytes 65552 | tf_op jit(solution)/shard_map/psum | solution.py:173
  933.6 1.5 broadcast_multiply_fusion.1
  (90 shorter events, 7.4 us)
Async XLA Ops:
  7.2 85.3 %copy-start = (f32[4,4,5,128]{3,1,2,0:T(4,128)S(1)}, f32[4,4,5,128]{3,1,2,0:T(4,128)}, u32[]{:S(2)}) copy-start(f32[4,4,5,128]{3,1,2,0:T(4,128)} %param.25) | copy-start | bytes 122884
  7.2 15.3 %copy-start.19 = (s32[5]{0:T(128)S(1)}, s32[5]{0:T(128)}, u32[]{:S(2)}) copy-start(s32[5]{0:T(128)} %constant.246.clone) | copy-start | bytes 64
  7.2 15.3 %copy-start.20 = (s32[5]{0:T(128)S(1)}, s32[5]{0:T(128)}, u32[]{:S(2)}) copy-start(s32[5]{0:T(128)} %constant.247.clone) | copy-start | bytes 64
  7.2 15.3 %copy-start.18 = (s32[4,2]{0,1:T(2,128)S(1)}, s32[4,2]{0,1:T(2,128)}, u32[]{:S(2)}) copy-start(s32[4,2]{0,1:T(2,128)} %param.27) | copy-start | bytes 100
  7.2 15.5 %copy-start.16 = (f32[6,6,128]{2,1,0:T(8,128)S(1)}, f32[6,6,128]{2,1,0:T(8,128)}, u32[]{:S(2)}) copy-start(f32[6,6,128]{2,1,0:T(8,128)} %param.24) | copy-start | bytes 55300
  7.2 323.1 %all-gather.2.cloned.1.call-start = ((), (), s32[]{:S(2)}) async-start(), calls=%async_computation | async-start | bytes 2949120 | tf_op jit(solution)/shard_map/all_gather | solution.py:168
  7.3 27.5 %collective-permute-start = (f32[64,6,6,128]{3,0,2,1:T(8,128)}, f32[64,6,6,128]{3,0,2,1:T(8,128)S(1)}, u32[]{:S(2)}, u32[]{:S(2)}) collective-permute-start(f32[64,6,6,128]{3,0,2,1:T(8,128)} %param.23), channel_id=1, source_target_pairs={{16,0},{32,16},{48,32},{17,1},{33,17},{49,33},{18,2},{34,18},{50,3... | collective-permute-start | bytes 3538952 | tf_op jit(solution)/shard_map/ppermute | solution.py:37
  8.6 27.2 %collective-permute-start.1 = (f32[64,6,6,128]{3,0,2,1:T(8,128)}, f32[64,6,6,128]{3,0,2,1:T(8,128)S(1)}, u32[]{:S(2)}, u32[]{:S(2)}) collective-permute-start(f32[64,6,6,128]{3,0,2,1:T(8,128)} %param.23), channel_id=1, source_target_pairs={{0,16},{16,32},{32,48},{1,17},{17,33},{33,49},{2,18},{18,34},{34,5... | collective-permute-start | bytes 3538952 | tf_op jit(solution)/shard_map/ppermute | solution.py:35
  13.2 28.1 %collective-permute-start.3 = (f32[64,6,6,128]{3,0,2,1:T(8,128)}, f32[64,6,6,128]{3,0,2,1:T(8,128)}, u32[]{:S(2)}, u32[]{:S(2)}) collective-permute-start(f32[64,6,6,128]{3,0,2,1:T(8,128)} %param.23), channel_id=1, source_target_pairs={{0,1},{1,2},{2,3},{3,4},{4,5},{5,6},{6,7},{7,8},{8,9},{9,10},{10,1... | collective-permute-start | bytes 3538952 | tf_op jit(solution)/shard_map/ppermute | solution.py:35
  18.1 53.6 %collective-permute-start.2 = (f32[64,6,6,128]{3,0,2,1:T(8,128)}, f32[64,6,6,128]{3,0,2,1:T(8,128)}, u32[]{:S(2)}, u32[]{:S(2)}) collective-permute-start(f32[64,6,6,128]{3,0,2,1:T(8,128)} %param.23), channel_id=1, source_target_pairs={{1,0},{2,1},{3,2},{4,3},{5,4},{6,5},{7,6},{8,7},{9,8},{10,9},{11,1... | collective-permute-start | bytes 3538952 | tf_op jit(solution)/shard_map/ppermute | solution.py:37
  34.8 2.0 copy-start.8
  35.8 1.1 copy-start.10
  36.9 6.5 copy-start.3
  89.8 2.6 copy-start.17
  96.6 16.4 %collective-permute-start.4 = (bf16[64,6,128]{2,0,1:T(8,128)(2,1)S(1)}, bf16[64,6,128]{2,0,1:T(8,128)(2,1)S(1)}, u32[]{:S(2)}, u32[]{:S(2)}) collective-permute-start(bf16[64,6,128]{2,0,1:T(8,128)(2,1)S(1)} %get-tuple-element.122), channel_id=1, source_target_pairs={{16,0},{32,16},{48,32},{17,1},{33,17},{49,33},{18,2},{34,18},{50,3... | collective-permute-start | bytes 294920 | tf_op jit(solution)/shard_map/ppermute | solution.py:24
  98.9 10.4 %copy-start.9 = (f32[64,6,6,128]{3,0,2,1:T(8,128)S(1)}, f32[64,6,6,128]{3,0,2,1:T(8,128)}, u32[]{:S(2)}) copy-start(f32[64,6,6,128]{3,0,2,1:T(8,128)} %copy-done.8) | copy-start | bytes 3538948
  99.2 12.1 %copy-start.11 = (f32[64,6,6,128]{3,0,2,1:T(8,128)S(1)}, f32[64,6,6,128]{3,0,2,1:T(8,128)}, u32[]{:S(2)}) copy-start(f32[64,6,6,128]{3,0,2,1:T(8,128)} %copy-done.10) | copy-start | bytes 3538948
  99.2 15.7 %collective-permute-start.5 = (bf16[64,6,128]{2,0,1:T(8,128)(2,1)S(1)}, bf16[64,6,128]{2,0,1:T(8,128)(2,1)S(1)}, u32[]{:S(2)}, u32[]{:S(2)}) collective-permute-start(bf16[64,6,128]{2,0,1:T(8,128)(2,1)S(1)} %get-tuple-element.121), channel_id=1, source_target_pairs={{0,16},{16,32},{32,48},{1,17},{17,33},{33,49},{2,18},{18,34},{34,5... | collective-permute-start | bytes 294920 | tf_op jit(solution)/shard_map/ppermute | solution.py:24
  103.3 17.9 %collective-permute-start.6 = (f32[64,6,128]{2,1,0:T(8,128)}, f32[64,6,128]{2,1,0:T(8,128)}, u32[]{:S(2)}, u32[]{:S(2)}) collective-permute-start(f32[64,6,128]{2,1,0:T(8,128)} %get-tuple-element.111), channel_id=1, source_target_pairs={{1,0},{2,1},{3,2},{4,3},{5,4},{6,5},{7,6},{8,7},{9,8},{10,9},{11,1... | collective-permute-start | bytes 589832 | tf_op jit(solution)/shard_map/ppermute | solution.py:24
  104.6 18.4 %collective-permute-start.7 = (f32[64,6,128]{2,1,0:T(8,128)}, f32[64,6,128]{2,1,0:T(8,128)}, u32[]{:S(2)}, u32[]{:S(2)}) collective-permute-start(f32[64,6,128]{2,1,0:T(8,128)} %get-tuple-element.110), channel_id=1, source_target_pairs={{0,1},{1,2},{2,3},{3,4},{4,5},{5,6},{6,7},{7,8},{8,9},{9,10},{10,1... | collective-permute-start | bytes 589832 | tf_op jit(solution)/shard_map/ppermute | solution.py:24
  159.5 11.9 %copy-start.1 = (f32[64,6,6,128]{3,1,0,2:T(8,128)}, f32[64,6,6,128]{3,1,0,2:T(8,128)S(1)}, u32[]{:S(2)}) copy-start(f32[64,6,6,128]{3,1,0,2:T(8,128)S(1)} %get-tuple-element.106) | copy-start | bytes 3538948
  159.7 27.7 %collective-permute-start.8 = (f32[64,6,6,128]{3,0,2,1:T(8,128)S(1)}, f32[64,6,6,128]{3,0,2,1:T(8,128)S(1)}, u32[]{:S(2)}, u32[]{:S(2)}) collective-permute-start(f32[64,6,6,128]{3,0,2,1:T(8,128)S(1)} %copy.104), channel_id=1, source_target_pairs={{16,0},{32,16},{48,32},{17,1},{33,17},{49,33},{18,2},{34,18},{50,3... | collective-permute-start | bytes 3538952 | tf_op jit(solution)/shard_map/ppermute | solution.py:37
  161.0 28.0 %collective-permute-start.10 = (f32[64,6,6,128]{3,0,2,1:T(8,128)S(1)}, f32[64,6,6,128]{3,0,2,1:T(8,128)S(1)}, u32[]{:S(2)}, u32[]{:S(2)}) collective-permute-start(f32[64,6,6,128]{3,0,2,1:T(8,128)S(1)} %copy.104), channel_id=1, source_target_pairs={{1,0},{2,1},{3,2},{4,3},{5,4},{6,5},{7,6},{8,7},{9,8},{10,9},{11,1... | collective-permute-start | bytes 3538952 | tf_op jit(solution)/shard_map/ppermute | solution.py:37
  162.3 27.4 %collective-permute-start.11 = (f32[64,6,6,128]{3,0,2,1:T(8,128)S(1)}, f32[64,6,6,128]{3,0,2,1:T(8,128)S(1)}, u32[]{:S(2)}, u32[]{:S(2)}) collective-permute-start(f32[64,6,6,128]{3,0,2,1:T(8,128)S(1)} %copy.104), channel_id=1, source_target_pairs={{0,1},{1,2},{2,3},{3,4},{4,5},{5,6},{6,7},{7,8},{8,9},{9,10},{10,1... | collective-permute-start | bytes 3538952 | tf_op jit(solution)/shard_map/ppermute | solution.py:35
  166.4 26.7 %collective-permute-start.9 = (f32[64,6,6,128]{3,0,2,1:T(8,128)S(1)}, f32[64,6,6,128]{3,0,2,1:T(8,128)S(1)}, u32[]{:S(2)}, u32[]{:S(2)}) collective-permute-start(f32[64,6,6,128]{3,0,2,1:T(8,128)S(1)} %copy.104), channel_id=1, source_target_pairs={{0,16},{16,32},{32,48},{1,17},{17,33},{33,49},{2,18},{18,34},{34,5... | collective-permute-start | bytes 3538952 | tf_op jit(solution)/shard_map/ppermute | solution.py:35
  187.4 1.1 copy-start.12
  189.8 1.5 copy-start.5
  190.5 3.7 copy-start.6
  193.1 1.2 copy-start.14
  206.0 16.8 %collective-permute-start.12 = (bf16[64,6,128]{2,0,1:T(8,128)(2,1)S(1)}, bf16[64,6,128]{2,0,1:T(8,128)(2,1)S(1)}, u32[]{:S(2)}, u32[]{:S(2)}) collective-permute-start(bf16[64,6,128]{2,0,1:T(8,128)(2,1)S(1)} %get-tuple-element.120), channel_id=1, source_target_pairs={{16,0},{32,16},{48,32},{17,1},{33,17},{49,33},{18,2},{34,18},{50,3... | collective-permute-start | bytes 294920 | tf_op jit(solution)/shard_map/ppermute | solution.py:24
  208.3 10.7 %copy-start.13 = (f32[64,6,6,128]{3,0,2,1:T(8,128)S(1)}, f32[64,6,6,128]{3,0,2,1:T(8,128)}, u32[]{:S(2)}) copy-start(f32[64,6,6,128]{3,0,2,1:T(8,128)} %copy-done.12) | copy-start | bytes 3538948
  208.6 12.4 %copy-start.15 = (f32[64,6,6,128]{3,0,2,1:T(8,128)S(1)}, f32[64,6,6,128]{3,0,2,1:T(8,128)}, u32[]{:S(2)}) copy-start(f32[64,6,6,128]{3,0,2,1:T(8,128)} %copy-done.14) | copy-start | bytes 3538948
  208.6 16.2 %collective-permute-start.13 = (bf16[64,6,128]{2,0,1:T(8,128)(2,1)S(1)}, bf16[64,6,128]{2,0,1:T(8,128)(2,1)S(1)}, u32[]{:S(2)}, u32[]{:S(2)}) collective-permute-start(bf16[64,6,128]{2,0,1:T(8,128)(2,1)S(1)} %get-tuple-element.119), channel_id=1, source_target_pairs={{0,16},{16,32},{32,48},{1,17},{17,33},{33,49},{2,18},{18,34},{34,5... | collective-permute-start | bytes 294920 | tf_op jit(solution)/shard_map/ppermute | solution.py:24
  213.4 17.7 %collective-permute-start.14 = (f32[64,6,128]{2,1,0:T(8,128)}, f32[64,6,128]{2,1,0:T(8,128)S(1)}, u32[]{:S(2)}, u32[]{:S(2)}) collective-permute-start(f32[64,6,128]{2,1,0:T(8,128)} %get-tuple-element.109), channel_id=1, source_target_pairs={{1,0},{2,1},{3,2},{4,3},{5,4},{6,5},{7,6},{8,7},{9,8},{10,9},{11,1... | collective-permute-start | bytes 589832 | tf_op jit(solution)/shard_map/ppermute | solution.py:24
  214.7 18.1 %collective-permute-start.15 = (f32[64,6,128]{2,1,0:T(8,128)}, f32[64,6,128]{2,1,0:T(8,128)S(1)}, u32[]{:S(2)}, u32[]{:S(2)}) collective-permute-start(f32[64,6,128]{2,1,0:T(8,128)} %get-tuple-element.108), channel_id=1, source_target_pairs={{0,1},{1,2},{2,3},{3,4},{4,5},{5,6},{6,7},{7,8},{8,9},{9,10},{10,1... | collective-permute-start | bytes 589832 | tf_op jit(solution)/shard_map/ppermute | solution.py:24
  224.7 9.8 %copy-start.2 = (f32[64,6,6,128]{3,1,0,2:T(8,128)S(1)}, f32[64,6,6,128]{3,1,0,2:T(8,128)}, u32[]{:S(2)}) copy-start(f32[64,6,6,128]{3,1,0,2:T(8,128)} %copy-done.1) | copy-start | bytes 3538948
  224.7 9.8 %copy-start.4 = (f32[64,6,6,128]{3,0,2,1:T(8,128)S(1)}, f32[64,6,6,128]{3,0,2,1:T(8,128)}, u32[]{:S(2)}) copy-start(f32[64,6,6,128]{3,0,2,1:T(8,128)} %param.23) | copy-start | bytes 3538948
  251.9 81.8 %copy-start.7 = (f32[64,6,6,128]{3,1,0,2:T(8,128)S(1)}, f32[64,6,6,128]{3,1,0,2:T(8,128)}, u32[]{:S(2)}) copy-start(f32[64,6,6,128]{3,1,0,2:T(8,128)} %get-tuple-element.105) | copy-start | bytes 3538948
  252.0 681.7 %all-reduce.4.cloned.1.call-start = ((), (), s32[]{:S(2)}) async-start(), calls=%async_computation.1 | async-start | bytes 131072 | tf_op jit(solution)/shard_map/psum | solution.py:173
Sparse Core Ops, SparseCore 0:
  252.1 78.2 all-gather.1
  333.8 599.7 all-reduce.3
where the time goes:
time: 957 us; the launch traced here: 942 us
  waiting for transfers between devices  738 us (77%)
  local copies, waits for them, and re-layouts  71.5 us (7%)
  other arithmetic  58.9 us (6%)
  starting transfers between devices  46.2 us (5%)
  between operations  14.6 us (2%)
  matrix products  12.6 us (1%)
    psum x1, waiting for transfers between devices, local(): gram = lax.psum(partial_rows, ('sx', 'sy')) / cell_total  599 us
    all_gather x1, waiting for transfers between devices, local(): lax.all_gather(flat, 'band', axis=0, tiled=True)  78.4 us
    ppermute x4, waiting for transfers between devices, extended(): lax.ppermute(head, axis, [((i + 1) % count, i) for i in range(ends)])  54.4 us
    div x1, other arithmetic, local(): current = (apply_h(orbitals) - filter_center * orbitals) / filter_half  34.7 us
    ppermute x8, starting transfers between devices, from_behind(): return lax.ppermute(block, axis, route)  23.1 us
    concatenate x2, local copies, waits for them, and re-layouts, nonlocal_term(): jnp.concatenate([field.reshape(batch, inner, count_z), ext_x[:, 5], ext_x...  20.6 us
  transfers between devices with their start and end apart: 18, of which 9 were waited for; matrix products, arithmetic and copies ran while one was open for 5% of the time, Pallas kernels for 0%

commit v1 on v0

v1 whole, which is shorter than its diff:
```python
import functools

import jax
import jax.numpy as jnp
from jax import lax
from jax.experimental import pallas as pl
from jax.experimental.pallas import tpu as pltpu
from jax.sharding import PartitionSpec as P

F32 = jnp.float32
BF16 = jnp.bfloat16
MESH = pl.DeviceIdType.MESH

stencil_weights = (
    -5369.0 / 1800.0,
    12.0 / 7.0,
    -15.0 / 56.0,
    10.0 / 189.0,
    -1.0 / 112.0,
    2.0 / 1925.0,
    -1.0 / 16632.0,
)
filter_center = 6.5
filter_half = 6.0

ORB = 64
CHUNKS = 2
ROWS = ORB // CHUNKS
SUB = 16
CELLS = 36
HALF = CELLS // 2
SRC_ROWS = 24
MSG_ROWS = 6 * SRC_ROWS
NT = (((1,), (1,)), ((), ()))
NN = (((1,), (0,)), ((), ()))


def dot(a, b, dims=NN):
    return lax.dot_general(a, b, dims, preferred_element_type=F32)


def split(value):
    high = value.astype(BF16)
    return high, (value - high.astype(F32)).astype(BF16)


def kernel(
    cells_total,
    y0,
    pot,
    proj,
    energies,
    centers,
    out,
    gram,
    y1,
    zn,
    msg,
    weights,
    banded,
    sent,
    halo,
    part,
    part_in,
    coef,
    energy,
    own,
    mate_in,
    far_in,
    cross_in,
    flip,
    flip_in,
    sums,
    scat_in,
    deep,
    deep_in,
    whole,
    s_msg,
    r_msg,
    s_halo,
    r_halo,
    s_part,
    r_part,
    s_coef,
    r_coef,
    s_mate,
    r_mate,
    s_far,
    r_far,
    s_cross,
    r_cross,
    s_flip,
    r_flip,
    s_scat,
    r_scat,
    s_deep,
    r_deep,
    s_whole,
    r_whole,
):
    ix, iy, ib = lax.axis_index("sx"), lax.axis_index("sy"), lax.axis_index("band")
    group, core = ib // 2, lax.rem(ib, 2)
    row_y, low_z = iy // 4, lax.rem(iy, 4)
    plane = ix * 4 + row_y
    near = ({"sx": ix - 1}, {"sx": ix + 1}, {"sy": iy - 1}, {"sy": iy + 1})
    has = (ix > 0, ix < 3, iy > 0, iy < 15)
    mate = {"band": group * 2 + (1 - core)}
    far = {"band": (1 - group) * 2 + core}
    cross = {"band": (1 - group) * 2 + (1 - core)}

    def plane_peer(step):
        other = lax.rem(plane + step, 16)
        return other, {"sx": other // 4, "sy": lax.rem(other, 4) * 4 + low_z}

    def deep_peer(step):
        other = lax.rem(low_z + step, 4)
        return other, {"sy": row_y * 4 + other}

    def remote(src, dst, send, recv, device):
        return pltpu.make_async_remote_copy(
            src_ref=src,
            dst_ref=dst,
            send_sem=send,
            recv_sem=recv,
            device_id=device,
            device_id_type=MESH,
        )

    barrier = pltpu.get_barrier_semaphore()

    def greet(device):
        pl.semaphore_signal(barrier, inc=1, device_id=device, device_id_type=MESH)

    greet({"sx": lax.rem(ix + 1, 4)})
    greet({"sx": lax.rem(ix + 3, 4)})
    greet({"sy": lax.rem(iy + 1, 16)})
    greet({"sy": lax.rem(iy + 15, 16)})
    greet(mate)
    greet(far)
    greet(cross)

    @pl.loop(1, 16)
    def _(step):
        greet(plane_peer(step)[1])

    @pl.loop(1, 4)
    def _(step):
        greet(deep_peer(step)[1])

    line = lax.broadcasted_iota(jnp.int32, (SRC_ROWS, 128), 0)
    atom = line // 5
    tile = line - atom * 5
    shift_x = jnp.where(tile == 1, -1, jnp.where(tile == 2, 1, 0))
    shift_y = jnp.where(tile == 3, -1, jnp.where(tile == 4, 1, 0))
    cell_x = jnp.full((SRC_ROWS, 128), -1000, jnp.int32)
    cell_y = jnp.full((SRC_ROWS, 128), -1000, jnp.int32)
    for a in range(4):
        cell_x = jnp.where(atom == a, centers[a, 0], cell_x)
        cell_y = jnp.where(atom == a, centers[a, 1], cell_y)
    msg[0, 4 * SRC_ROWS : 5 * SRC_ROWS, :] = (cell_x + shift_x).astype(F32)
    msg[0, 5 * SRC_ROWS : 6 * SRC_ROWS, :] = (cell_y + shift_y).astype(F32)
    for p in range(4):
        for a in range(4):
            msg[0, p * SRC_ROWS + 5 * a : p * SRC_ROWS + 5 * a + 5, :] = proj[a, :, p, :]
        msg[0, p * SRC_ROWS + 20 : (p + 1) * SRC_ROWS, :] = jnp.zeros((4, 128), F32)

    pl.semaphore_wait(barrier, 7 + 15 + 3)

    def msg_copy(s):
        return remote(msg.at[0], msg.at[1 + (s ^ 1)], s_msg.at[s], r_msg.at[s ^ 1], near[s])

    def halo_copy(phase, c, s):
        return remote(
            sent.at[phase, c],
            halo.at[phase, c, s ^ 1],
            s_halo.at[phase, c, s],
            r_halo.at[phase, c, s ^ 1],
            near[s],
        )

    def part_copy(phase, c, s):
        return remote(
            part.at[phase, c, 1 + s],
            part_in.at[phase, c, s ^ 1],
            s_part.at[phase, c, s],
            r_part.at[phase, c, s ^ 1],
            near[s],
        )

    def coef_copy(phase, c, s):
        return remote(
            coef.at[phase, c, 0],
            coef.at[phase, c, 1 + (s ^ 1)],
            s_coef.at[phase, c, s],
            r_coef.at[phase, c, s ^ 1],
            near[s],
        )

    def start_all(copy, *index):
        for s in range(4):

            @pl.when(has[s])
            def _(s=s):
                copy(*index, s).start()

    def arrive_all(copy, *index):
        for s in range(4):

            @pl.when(has[s])
            def _(s=s):
                copy(*index, s ^ 1).wait_recv()

    def sent_all(copy, *index):
        for s in range(4):

            @pl.when(has[s])
            def _(s=s):
                copy(*index, s).wait_send()

    start_all(msg_copy)

    def rows_of(c):
        return pl.ds(pl.multiple_of(c * ROWS, ROWS), ROWS)

    def send_first(c):
        for x in range(6):
            sent[0, c, 6 * x : 6 * x + 6] = y0[6 * x : 6 * x + 6, rows_of(c), :].astype(BF16)
        start_all(halo_copy, 0, c)

    send_first(0)

    for s in range(4):

        @pl.when(jnp.logical_not(has[s]))
        def _(s=s):
            msg[1 + s] = jnp.full((MSG_ROWS, 128), -1000.0, F32)
            msg[1 + s, : 4 * SRC_ROWS] = jnp.zeros((4 * SRC_ROWS, 128), F32)
            for phase in range(2):
                for c in range(CHUNKS):
                    halo[phase, c, s] = jnp.zeros((CELLS, ROWS, 128), BF16)
                    part_in[phase, c, s] = jnp.zeros((16, 128), F32)
                    coef[phase, c, 1 + s] = jnp.zeros((16, 128), F32)

    for phase in range(2):
        for c in range(CHUNKS):
            for s in range(5):
                part[phase, c, s] = jnp.zeros((16, 128), F32)

    distance = jnp.abs(
        lax.broadcasted_iota(jnp.int32, (128, 128), 0)
        - lax.broadcasted_iota(jnp.int32, (128, 128), 1)
    )
    band = jnp.zeros((128, 128), F32)
    for step in range(1, 7):
        band = jnp.where(distance == step, -0.5 * stencil_weights[step], band)
    band_high, band_low = split(band)
    banded[0:128, :] = band_high
    banded[128:256, :] = band_high
    banded[256:384, :] = band_low

    slot16 = lax.broadcasted_iota(jnp.int32, (16, 128), 0)
    level = jnp.zeros((16, 128), F32)
    for p in range(4):
        for a in range(4):
            level = jnp.where(slot16 == 4 * p + a, energies[a, p], level)
    energy[...] = level

    arrive_all(msg_copy)
    first_x, first_y = (ix * 6).astype(F32), (iy * 6).astype(F32)
    keys = []
    for s in range(5):
        local_x = msg[s, 4 * SRC_ROWS : 5 * SRC_ROWS, :] - first_x
        local_y = msg[s, 5 * SRC_ROWS : 6 * SRC_ROWS, :] - first_y
        inside = (local_x >= 0) & (local_x < 6) & (local_y >= 0) & (local_y < 6)
        place = (local_x * 6 + local_y) * 80 + (16 * s + atom).astype(F32)
        keys.append(jnp.where(inside & (line < 20), place, -1000.0))
    keys.append(jnp.full((8, 128), -1000.0, F32))
    key = jnp.concatenate(keys, axis=0).T[0:1, :]
    tables = []
    for p in range(4):
        stacked = [msg[s, p * SRC_ROWS : (p + 1) * SRC_ROWS, :] for s in range(5)]
        table = jnp.concatenate(stacked + [jnp.zeros((8, 128), F32)], axis=0)
        tables.append(jnp.concatenate(split(table), axis=1))
    table = jnp.concatenate(tables, axis=0)

    @pl.loop(0, 9)
    def _(block):
        row = lax.broadcasted_iota(jnp.int32, (320, 128), 0) + block * 320
        row = row.astype(F32)
        masks = [
            jnp.where(row == key + 4.0 * p, 1.0, 0.0).astype(BF16) for p in range(4)
        ]
        placed = dot(jnp.concatenate(masks, axis=1), table)
        placed = placed.reshape(4, 80, 256).astype(BF16)
        weights[pl.ds(block * 4, 4), 0:80, :] = placed[:, :, :128]
        weights[pl.ds(block * 4, 4), 80:160, :] = placed[:, :, :128]
        weights[pl.ds(block * 4, 4), 160:240, :] = placed[:, :, 128:]

    def partial(phase, c, source):
        def step(cell, total):
            high, low = split(source(cell))
            w_high, w_low = weights[cell, 0:80, :], weights[cell, 160:240, :]
            left = jnp.concatenate([w_high, w_low, w_high], axis=1)
            right = jnp.concatenate([high, high, low], axis=1)
            return total + dot(left, right, NT)

        total = lax.fori_loop(0, CELLS, step, jnp.zeros((80, ROWS), F32))
        for s in range(5):
            part[phase, c, s, :, 0:ROWS] = total[16 * s : 16 * s + 16, :]
        start_all(part_copy, phase, c)

    def finish_coef(phase, c):
        arrive_all(part_copy, phase, c)
        total = part[phase, c, 0]
        for s in range(4):
            total = total + part_in[phase, c, s]
        coef[phase, c, 0] = total * energy[...]
        start_all(coef_copy, phase, c)

    def along_z(source):
        for x in range(6):
            high, low = split(source(x).reshape(6 * ROWS, 128))
            left = jnp.concatenate([high, low, high], axis=1)
            zn[6 * x : 6 * x + 6] = dot(left, banded[...]).reshape(6, ROWS, 128)

    def projected(phase, c):
        arrive_all(coef_copy, phase, c)
        stacked = jnp.concatenate([coef[phase, c, s] for s in range(5)], axis=0)
        high = stacked.astype(BF16).astype(F32)
        low = (stacked - high).astype(BF16).astype(F32)
        left = jnp.concatenate([high, low, high], axis=0).T[0:ROWS, :].astype(BF16)

        @pl.loop(0, CELLS)
        def _(cell):
            zn[cell] += dot(left, weights[cell])

    center = -1.5 * stencil_weights[0] - filter_center

    def stencil(phase, c, source, finish):
        @pl.loop(0, ROWS // SUB)
        def _(block):
            rows = pl.ds(pl.multiple_of(block * SUB, SUB), SUB)
            for x in range(6):

                def layer(other):
                    if other < 0:
                        return halo[phase, c, 0, 6 * (other + 6) : 6 * (other + 7), rows, :].astype(F32)
                    if other > 5:
                        return halo[phase, c, 1, 6 * (other - 6) : 6 * (other - 5), rows, :].astype(F32)
                    return source(other, block)

                here = source(x, block)
                line_y = jnp.concatenate(
                    [
                        halo[phase, c, 2, 6 * x : 6 * x + 6, rows, :].astype(F32),
                        here,
                        halo[phase, c, 3, 6 * x : 6 * x + 6, rows, :].astype(F32),
                    ],
                    axis=0,
                )
                total = zn[6 * x : 6 * x + 6, rows, :]
                total = total + here * (pot[x][:, None, :] + center)
                for step in range(1, 7):
                    weight = -0.5 * stencil_weights[step]
                    pair = layer(x - step) + layer(x + step)
                    pair = pair + line_y[6 - step : 12 - step] + line_y[6 + step : 12 + step]
                    total = total + weight * pair
                finish(x, block, total)

    def block_rows(c, block):
        return pl.ds(pl.multiple_of(c * ROWS + block * SUB, SUB), SUB)

    for c in range(CHUNKS):
        partial(0, c, lambda cell, c=c: y0[cell, rows_of(c), :])
    for c in range(1, CHUNKS):
        send_first(c)
    for c in range(CHUNKS):
        finish_coef(0, c)

    @pl.loop(0, CHUNKS)
    def _(c):
        along_z(lambda x: y0[6 * x : 6 * x + 6, rows_of(c), :])
        projected(0, c)
        arrive_all(halo_copy, 0, c)

        def finish(x, block, total):
            value = total * (1.0 / filter_half)
            y1[c, 6 * x : 6 * x + 6, pl.ds(pl.multiple_of(block * SUB, SUB), SUB), :] = value
            sent[1, c, 6 * x : 6 * x + 6, pl.ds(pl.multiple_of(block * SUB, SUB), SUB), :] = (
                value.astype(BF16)
            )

        stencil(
            0, c, lambda x, block: y0[6 * x : 6 * x + 6, block_rows(c, block), :], finish
        )
        start_all(halo_copy, 1, c)
        partial(1, c, lambda cell: y1[c, cell])

    @pl.loop(0, CHUNKS)
    def _(c):
        finish_coef(1, c)

    def mate_copy(c):
        return remote(own.at[c], mate_in.at[c], s_mate.at[c], r_mate.at[c], mate)

    def far_copy(c):
        start = pl.multiple_of(group * HALF, HALF)
        return remote(
            own.at[c, pl.ds(start, HALF)], far_in.at[c], s_far.at[c], r_far.at[c], far
        )

    def cross_copy(c):
        return remote(far_in.at[c], cross_in.at[c], s_cross.at[c], r_cross.at[c], mate)

    @pl.loop(0, CHUNKS)
    def _(c):
        along_z(lambda x: y1[c, 6 * x : 6 * x + 6])
        projected(1, c)
        arrive_all(halo_copy, 1, c)

        def finish(x, block, total):
            before = y0[6 * x : 6 * x + 6, block_rows(c, block), :]
            value = total * (2.0 / filter_half) - before
            out[6 * x : 6 * x + 6, block_rows(c, block), :] = value
            own[c, 6 * x : 6 * x + 6, pl.ds(pl.multiple_of(block * SUB, SUB), SUB), :] = (
                value.astype(BF16)
            )

        stencil(
            1,
            c,
            lambda x, block: y1[
                c, 6 * x : 6 * x + 6, pl.ds(pl.multiple_of(block * SUB, SUB), SUB), :
            ],
            finish,
        )
        far_copy(c).start()
        mate_copy(c).start()

    @pl.loop(0, CHUNKS)
    def _(c):
        far_copy(c).wait_recv()
        cross_copy(c).start()

    @pl.loop(0, CHUNKS)
    def _(c):
        mate_copy(c).wait_recv()

    def gather(ref, cell):
        return jnp.concatenate([ref[c, cell] for c in range(CHUNKS)], axis=0)

    def in_order(first, second):
        return jnp.concatenate(
            [jnp.where(core == 0, first, second), jnp.where(core == 0, second, first)], axis=0
        )

    def near_step(cell, total):
        mine = gather(own, cell)
        return total + dot(mine, in_order(mine, gather(mate_in, cell)), NT)

    near_sum = lax.fori_loop(0, CELLS, near_step, jnp.zeros((ORB, 128), F32))

    @pl.loop(0, CHUNKS)
    def _(c):
        cross_copy(c).wait_recv()

    def far_step(cell, totals):
        mine = gather(own, (1 - group) * HALF + cell)
        theirs, others = gather(far_in, cell), gather(cross_in, cell)
        straight = totals[0] + dot(mine, in_order(theirs, others), NT)
        both = jnp.concatenate([theirs, others], axis=0)
        zero = jnp.zeros_like(mine)
        turned = totals[1] + dot(both, in_order(mine, zero), NT)
        return straight, turned

    far_sum, turned = lax.fori_loop(
        0, HALF, far_step, (jnp.zeros((ORB, 128), F32), jnp.zeros((2 * ORB, 128), F32))
    )
    flip[0] = turned[:ORB]
    flip[1] = turned[ORB:]
    flip_far = remote(flip.at[0], flip_in.at[0], s_flip.at[0], r_flip.at[0], far)
    flip_cross = remote(flip.at[1], flip_in.at[1], s_flip.at[1], r_flip.at[1], cross)
    flip_far.start()
    flip_cross.start()
    sums[0:ORB] = near_sum
    flip_far.wait_recv()
    flip_cross.wait_recv()
    sums[ORB : 2 * ORB] = far_sum + flip_in[0] + flip_in[1]

    def scat_copy(step):
        other, device = plane_peer(step)
        start = pl.multiple_of(other * 8, 8)
        return remote(
            sums.at[pl.ds(start, 8)], scat_in.at[step], s_scat.at[step], r_scat.at[step], device
        )

    def whole_copy(step):
        other, device = plane_peer(step)
        start = pl.multiple_of(plane * 8, 8)
        return remote(
            whole.at[pl.ds(start, 8)],
            whole.at[pl.ds(start, 8)],
            s_whole.at[step],
            r_whole.at[step],
            device,
        )

    def deep_copy(step):
        other, device = deep_peer(step)
        return remote(deep, deep_in.at[step], s_deep.at[step], r_deep.at[step], device)

    @pl.loop(1, 16)
    def _(step):
        scat_copy(step).start()

    def add_scat(step, total):
        scat_copy(step).wait_recv()
        return total + scat_in[step]

    mine = sums[pl.ds(pl.multiple_of(plane * 8, 8), 8), :]
    mine = lax.fori_loop(1, 16, add_scat, mine)
    deep[...] = mine
    for step in range(1, 4):
        deep_copy(step).start()
    for step in range(1, 4):
        deep_copy(step).wait_recv()
        mine = mine + deep_in[step]
    whole[pl.ds(pl.multiple_of(plane * 8, 8), 8), :] = mine * (1.0 / cells_total)

    @pl.loop(1, 16)
    def _(step):
        whole_copy(step).start()

    @pl.loop(1, 16)
    def _(step):
        other = lax.rem(plane + 16 - step, 16)
        start = pl.multiple_of(other * 8, 8)
        remote(
            whole.at[pl.ds(start, 8)],
            whole.at[pl.ds(start, 8)],
            s_whole.at[step],
            r_whole.at[step],
            plane_peer(step)[1],
        ).wait_recv()

    near_all, far_all = whole[0:ORB, :], whole[ORB : 2 * ORB, :]
    gram[:, 0:128] = jnp.where(group == 0, near_all, far_all)
    gram[:, 128:256] = jnp.where(group == 0, far_all, near_all)

    sent_all(msg_copy)
    for phase in range(2):

        @pl.loop(0, CHUNKS)
        def _(c, phase=phase):
            sent_all(halo_copy, phase, c)
            sent_all(part_copy, phase, c)
            sent_all(coef_copy, phase, c)

    @pl.loop(0, CHUNKS)
    def _(c):
        mate_copy(c).wait_send()
        far_copy(c).wait_send()
        cross_copy(c).wait_send()

    flip_far.wait_send()
    flip_cross.wait_send()

    @pl.loop(1, 16)
    def _(step):
        scat_copy(step).wait_send()
        whole_copy(step).wait_send()

    for step in range(1, 4):
        deep_copy(step).wait_send()


def local(orbitals, potential, projectors, energies, centers):
    y0 = orbitals.transpose(1, 2, 0, 3).reshape(CELLS, ORB, 128)
    proj = projectors.transpose(0, 2, 1, 3)
    cells_total = CELLS * 128 * lax.axis_size("sx") * lax.axis_size("sy")
    vmem = pl.BlockSpec(memory_space=pltpu.VMEM)
    smem = pl.BlockSpec(memory_space=pltpu.SMEM)
    dma = pltpu.SemaphoreType.DMA
    chunk = (CHUNKS, CELLS, ROWS, 128)
    half = (CHUNKS, HALF, ROWS, 128)
    out, gram = pl.pallas_call(
        functools.partial(kernel, cells_total),
        out_shape=(
            jax.ShapeDtypeStruct((CELLS, ORB, 128), F32),
            jax.ShapeDtypeStruct((ORB, 256), F32),
        ),
        in_specs=[vmem, vmem, vmem, smem, smem],
        out_specs=(vmem, vmem),
        scratch_shapes=[
            pltpu.VMEM(chunk, F32),
            pltpu.VMEM((CELLS, ROWS, 128), F32),
            pltpu.VMEM((5, MSG_ROWS, 128), F32),
            pltpu.VMEM((CELLS, 240, 128), BF16),
            pltpu.VMEM((384, 128), BF16),
            pltpu.VMEM((2,) + chunk, BF16),
            pltpu.VMEM((2, CHUNKS, 4, CELLS, ROWS, 128), BF16),
            pltpu.VMEM((2, CHUNKS, 5, 16, 128), F32),
            pltpu.VMEM((2, CHUNKS, 4, 16, 128), F32),
            pltpu.VMEM((2, CHUNKS, 5, 16, 128), F32),
            pltpu.VMEM((16, 128), F32),
            pltpu.VMEM(chunk, BF16),
            pltpu.VMEM(chunk, BF16),
            pltpu.VMEM(half, BF16),
            pltpu.VMEM(half, BF16),
            pltpu.VMEM((2, ORB, 128), F32),
            pltpu.VMEM((2, ORB, 128), F32),
            pltpu.VMEM((2 * ORB, 128), F32),
            pltpu.VMEM((16, 8, 128), F32),
            pltpu.VMEM((8, 128), F32),
            pltpu.VMEM((4, 8, 128), F32),
            pltpu.VMEM((2 * ORB, 128), F32),
            dma((4,)),
            dma((4,)),
            dma((2, CHUNKS, 4)),
            dma((2, CHUNKS, 4)),
            dma((2, CHUNKS, 4)),
            dma((2, CHUNKS, 4)),
            dma((2, CHUNKS, 4)),
            dma((2, CHUNKS, 4)),
            dma((CHUNKS,)),
            dma((CHUNKS,)),
            dma((CHUNKS,)),
            dma((CHUNKS,)),
            dma((CHUNKS,)),
            dma((CHUNKS,)),
            dma((2,)),
            dma((2,)),
            dma((16,)),
            dma((16,)),
            dma((4,)),
            dma((4,)),
            dma((16,)),
            dma((16,)),
        ],
        compiler_params=pltpu.CompilerParams(
            collective_id=0, has_side_effects=True, vmem_limit_bytes=48 * 1024 * 1024
        ),
        name="filter_and_gram",
    )(y0, potential, proj, energies, centers)
    filtered = out.reshape(6, 6, ORB, 128).transpose(2, 0, 1, 3)
    return filtered, gram


def solution(mesh):
    in_specs = (
        P("band", "sx", "sy", None),
        P("sx", "sy", None),
        P(("sx", "sy"), None, None, None),
        P(("sx", "sy"), None),
        P(("sx", "sy"), None),
    )
    out_specs = (P("band", "sx", "sy", None), P("band", None))
    return jax.shard_map(local, mesh=mesh, in_specs=in_specs, out_specs=out_specs, check_vma=False)
```

time: 957 us -> 136 us (0.14); the launches traced: 942 us -> 135 us
  waiting for transfers between devices: 738 us -> 0 us
  Pallas kernels: 0 us -> 129 us
  local copies, waits for them, and re-layouts: 71.5 us -> 5.88 us
  other arithmetic: 58.9 us -> 0 us
  starting transfers between devices: 46.2 us -> 0 us
  between operations: 14.6 us -> 0.64 us
  matrix products: 12.6 us -> 0 us
    psum x1 -> x0, waiting for transfers between devices: 599 us -> none  [local(): gram = lax.psum(partial_rows, ('sx', 'sy')) / cell_total]
    pallas_call x0 -> x1, Pallas kernels: none -> 129 us  [local(): pl.pallas_call(functools.partial(kernel, cells_total), out_shape=(jax.Sha...]
    all_gather x1 -> x0, waiting for transfers between devices: 78.4 us -> none  [local(): lax.all_gather(flat, 'band', axis=0, tiled=True)]
    ppermute x16 -> x0, waiting for transfers between devices: 61 us -> none  [the longest x4 54.4 us: extended(): lax.ppermute(head, axis, [((i + 1) % count, i) for i in range(ends)])]
    ppermute x16 -> x0, starting transfers between devices: 46.1 us -> none  [the longest x8 23.1 us: from_behind(): return lax.ppermute(block, axis, route)]
    div x2 -> x0, other arithmetic: 36.2 us -> none  [the longest x1 34.7 us: local(): current = (apply_h(orbitals) - filter_center * orbitals) / filter_half]
    concatenate x3 -> x0, local copies, waits for them, and re-layouts: 23.8 us -> none  [the longest x2 20.6 us: nonlocal_term(): jnp.concatenate([field.reshape(batch, inner, count_z), ext_x[:, 5], ext_x...]
    scatter-add x4 -> x0, local copies, waits for them, and re-layouts: 15.9 us -> none  [the longest x2 12.3 us: nonlocal_term(): result = result.at[:, 0].add(from_left)]
  transfers between devices with their start and end apart: 18 -> 0, of which waited for: 9 -> 0; matrix products, arithmetic and copies ran while one was open for 5% -> 0% of each run, Pallas kernels for 0% -> 0%
where the time goes in v1:
time: 136 us; the launch traced here: 135 us
  Pallas kernels  129 us (95%)
  local copies, waits for them, and re-layouts  5.88 us (4%)
    pallas_call x1, Pallas kernels, local(): pl.pallas_call(functools.partial(kernel, cells_total), out_shape=(jax.Sha...  129 us
    unnamed x11, local copies, waits for them, and re-layouts  5.88 us

profile of v1, /device:TPU:1, one launch (start us, length us, event | category | flops | bytes accessed | tf_op | source)
XLA Modules:
  0.0 135.1 jit_solution(11452220075451780012)
XLA Ops:
  0.6 0.8 copy.7.centers
  1.4 0.0 copy-start
  1.4 1.3 copy-done
  2.7 0.0 copy-start.1
  2.7 0.8 copy-done.1
  3.4 0.0 copy-start.2
  3.4 0.7 copy-done.2
  4.2 0.0 copy-start.3
  4.2 0.7 copy-done.3
  4.9 128.5 %filter_and_gram.1 = (f32[36,64,128]{2,1,0:T(8,128)S(1)}, f32[64,256]{1,0:T(8,128)S(1)}) custom-call(f32[36,64,128]{2,1,0:T(8,128)S(1)} %bitcast.7, f32[6,6,128]{2,1,0:T(8,128)S(1)} %copy-done.2, f32[4,5,4,128]{3,2,1,0:T(4,128)S(1)} %bitcast.9, f32[4,4]{1,0:T(4,128)S(1)} %copy-done.3, s32[4,2]{1,0:T(4,128)S(1)} %copy.7.centers), custom_call_target="tpu_custom_call" | custom-call | tf_op jit(solution)/shard_map/filter_and_gram/pallas_call | solution.py:586
  133.4 1.0 copy.10
  134.4 0.6 copy.11
Async XLA Ops:
  1.4 1.3 copy-start
  2.7 0.8 copy-start.1
  3.4 0.7 copy-start.2
  4.2 0.7 copy-start.3

commit v2 on v1

v2 whole, which is shorter than its diff:
```python
import functools

import jax
import jax.numpy as jnp
from jax import lax
from jax.experimental import pallas as pl
from jax.experimental.pallas import tpu as pltpu
from jax.sharding import PartitionSpec as P

F32 = jnp.float32
BF16 = jnp.bfloat16
MESH = pl.DeviceIdType.MESH

stencil_weights = (
    -5369.0 / 1800.0,
    12.0 / 7.0,
    -15.0 / 56.0,
    10.0 / 189.0,
    -1.0 / 112.0,
    2.0 / 1925.0,
    -1.0 / 16632.0,
)
filter_center = 6.5
filter_half = 6.0

ORB = 64
CHUNKS = 4
ROWS = ORB // CHUNKS
CELLS = 36
HALF = CELLS // 2
PAIRS = 20
MSG_ROWS = 4 * PAIRS + 8
GROUP = ORB // 2
NT = (((1,), (1,)), ((), ()))
NN = (((1,), (0,)), ((), ()))


def dot(a, b, dims=NN):
    return lax.dot_general(a, b, dims, preferred_element_type=F32)


def split(value):
    high = value.astype(BF16)
    return high, (value - high.astype(F32)).astype(BF16)


def kernel(
    cells_total,
    y0_hbm,
    pot_hbm,
    proj_hbm,
    energies,
    centers,
    out,
    gram,
    y0,
    pot,
    proj,
    y1,
    zn,
    msg,
    weights,
    banded,
    sent,
    halo,
    part,
    part_in,
    coef,
    energy,
    wide,
    own,
    mate_in,
    far_in,
    cross_in,
    sums,
    scat_in,
    deep,
    deep_in,
    turn_in,
    whole,
    s_load,
    s_msg,
    r_msg,
    s_halo,
    r_halo,
    s_part,
    r_part,
    s_coef,
    r_coef,
    s_mate,
    r_mate,
    s_far,
    r_far,
    s_cross,
    r_cross,
    s_scat,
    r_scat,
    s_deep,
    r_deep,
    s_turn,
    r_turn,
    s_whole,
    r_whole,
):
    ix, iy, ib = lax.axis_index("sx"), lax.axis_index("sy"), lax.axis_index("band")
    group, core = ib // 2, lax.rem(ib, 2)
    row_y, low_z = iy // 4, lax.rem(iy, 4)
    plane = ix * 4 + row_y
    near = ({"sx": ix - 1}, {"sx": ix + 1}, {"sy": iy - 1}, {"sy": iy + 1})
    has = (ix > 0, ix < 3, iy > 0, iy < 15)
    mate = {"band": group * 2 + (1 - core)}
    far = {"band": (1 - group) * 2 + core}
    cross = {"band": (1 - group) * 2 + (1 - core)}

    def plane_peer(step):
        other = lax.rem(plane + step, 16)
        return other, {"sx": other // 4, "sy": lax.rem(other, 4) * 4 + low_z}

    def deep_peer(step):
        other = lax.rem(low_z + step, 4)
        return other, {"sy": row_y * 4 + other}

    def remote(src, dst, send, recv, device):
        return pltpu.make_async_remote_copy(
            src_ref=src,
            dst_ref=dst,
            send_sem=send,
            recv_sem=recv,
            device_id=device,
            device_id_type=MESH,
        )

    loads = [
        pltpu.make_async_copy(proj_hbm, proj, s_load.at[0]),
        pltpu.make_async_copy(y0_hbm, y0, s_load.at[1]),
        pltpu.make_async_copy(pot_hbm, pot, s_load.at[2]),
    ]
    for load in loads:
        load.start()
    barrier = pltpu.get_barrier_semaphore()

    def greet(device):
        pl.semaphore_signal(barrier, inc=1, device_id=device, device_id_type=MESH)

    greet({"sx": lax.rem(ix + 1, 4)})
    greet({"sx": lax.rem(ix + 3, 4)})
    greet({"sy": lax.rem(iy + 1, 16)})
    greet({"sy": lax.rem(iy + 15, 16)})
    greet(mate)
    greet(far)
    greet(cross)

    @pl.loop(1, 16)
    def _(step):
        greet(plane_peer(step)[1])

    @pl.loop(1, 4)
    def _(step):
        device = deep_peer(step)[1]
        greet(device)
        greet({**device, **far})
        greet({**device, **cross})

    lane = lax.broadcasted_iota(jnp.int32, (8, 128), 1)
    atom = lane // 5
    tile = lane - atom * 5
    shift_x = jnp.where(tile == 1, -1, jnp.where(tile == 2, 1, 0))
    shift_y = jnp.where(tile == 3, -1, jnp.where(tile == 4, 1, 0))
    cell_x = jnp.full((8, 128), -1000, jnp.int32)
    cell_y = jnp.full((8, 128), -1000, jnp.int32)
    for a in range(4):
        cell_x = jnp.where(atom == a, centers[0, a], cell_x)
        cell_y = jnp.where(atom == a, centers[1, a], cell_y)
    line = lax.broadcasted_iota(jnp.int32, (8, 128), 0)
    cells = jnp.where(line == 0, cell_x + shift_x, cell_y + shift_y)
    msg[0, 4 * PAIRS : MSG_ROWS, :] = cells.astype(F32)
    loads[0].wait()
    for p in range(4):
        for a in range(4):
            start = p * PAIRS + 5 * a
            msg[0, start : start + 5, :] = proj[a, :, p, :]

    for s in range(4):

        @pl.when(jnp.logical_not(has[s]))
        def _(s=s):
            msg[1 + s] = jnp.zeros((MSG_ROWS, 128), F32)
            msg[1 + s, 4 * PAIRS : MSG_ROWS] = jnp.full((8, 128), -1000.0, F32)
            for phase in range(2):
                for c in range(CHUNKS):
                    halo[phase, c, s] = jnp.zeros((CELLS, ROWS, 128), BF16)
            for k in range(3):
                part_in[k, s] = jnp.zeros((8, 128), F32)
                coef[k, 1 + s] = jnp.zeros((8, 128), F32)

    wide[...] = jnp.zeros((80, 128), F32)

    distance = jnp.abs(
        lax.broadcasted_iota(jnp.int32, (128, 128), 0)
        - lax.broadcasted_iota(jnp.int32, (128, 128), 1)
    )
    band = jnp.zeros((128, 128), F32)
    for step in range(1, 7):
        band = jnp.where(distance == step, -0.5 * stencil_weights[step], band)
    band_high, band_low = split(band)
    banded[0:128, :] = band_high
    banded[128:256, :] = band_high
    banded[256:384, :] = band_low

    level = jnp.zeros((8, 128), F32)
    for p in range(4):
        for a in range(4):
            row = 4 * p + a
            here = (line == row % 8) & ((lane >= 64) == (row >= 8))
            level = jnp.where(here, energies[a, p], level)
    energy[...] = level

    def rows_of(c):
        return pl.ds(pl.multiple_of(c * ROWS, ROWS), ROWS)

    loads[1].wait()
    for c in range(CHUNKS):
        for x in range(6):
            sent[0, c, 6 * x : 6 * x + 6] = y0[6 * x : 6 * x + 6, rows_of(c), :].astype(BF16)

    pl.semaphore_wait(barrier, 7 + 15 + 9)

    def msg_copy(s):
        return remote(msg.at[0], msg.at[1 + (s ^ 1)], s_msg.at[s], r_msg.at[s ^ 1], near[s])

    def halo_copy(phase, c, s):
        return remote(
            sent.at[phase, c],
            halo.at[phase, c, s ^ 1],
            s_halo.at[phase, c, s],
            r_halo.at[phase, c, s ^ 1],
            near[s],
        )

    def part_copy(k, s):
        return remote(
            part.at[k, 1 + s], part_in.at[k, s ^ 1], s_part.at[k, s], r_part.at[k, s ^ 1], near[s]
        )

    def coef_copy(k, s):
        return remote(
            coef.at[k, 0], coef.at[k, 1 + (s ^ 1)], s_coef.at[k, s], r_coef.at[k, s ^ 1], near[s]
        )

    def start_all(copy, *index):
        for s in range(4):

            @pl.when(has[s])
            def _(s=s):
                copy(*index, s).start()

    def arrive_all(copy, *index):
        for s in range(4):

            @pl.when(has[s])
            def _(s=s):
                copy(*index, s ^ 1).wait_recv()

    def sent_all(copy, *index):
        for s in range(4):

            @pl.when(has[s])
            def _(s=s):
                copy(*index, s).wait_send()

    start_all(msg_copy)
    start_all(halo_copy, 0, 0)

    arrive_all(msg_copy)
    first_x, first_y = (ix * 6).astype(F32), (iy * 6).astype(F32)
    key = jnp.full((1, 128), -1000.0, F32)
    wide_atom = atom.astype(F32)
    for s in range(5):
        coords = msg[s, 4 * PAIRS : MSG_ROWS, :]
        local_x, local_y = coords[0:1] - first_x, coords[1:2] - first_y
        inside = (local_x >= 0) & (local_x < 6) & (local_y >= 0) & (local_y < 6)
        inside = inside & (lane[0:1] < PAIRS)
        place = (local_x * 6 + local_y) * 80 + (16.0 * s + wide_atom[0:1])
        place = jnp.broadcast_to(jnp.where(inside, place, -1000.0), (8, 128))
        moved = pltpu.roll(place, PAIRS * s, 1)[0:1] if s else place[0:1]
        mine = (lane[0:1] >= PAIRS * s) & (lane[0:1] < PAIRS * (s + 1))
        key = jnp.where(mine, moved, key)
    tables = []
    for p in range(4):
        stacked = [msg[s, p * PAIRS : (p + 1) * PAIRS, :] for s in range(5)]
        table = jnp.concatenate(stacked + [jnp.zeros((28, 128), F32)], axis=0)
        tables.append(jnp.concatenate(split(table), axis=1))
    table = jnp.concatenate(tables, axis=0)

    @pl.loop(0, 9, unroll=3)
    def _(block):
        row = lax.broadcasted_iota(jnp.int32, (320, 128), 0) + block * 320
        row = row.astype(F32)
        masks = [
            jnp.where(row == key + 4.0 * p, 1.0, 0.0).astype(BF16) for p in range(4)
        ]
        placed = dot(jnp.concatenate(masks, axis=1), table)
        placed = placed.reshape(4, 80, 256).astype(BF16)
        weights[pl.ds(block * 4, 4), 0:80, :] = placed[:, :, :128]
        weights[pl.ds(block * 4, 4), 80:160, :] = placed[:, :, :128]
        weights[pl.ds(block * 4, 4), 160:240, :] = placed[:, :, 128:]

    def partial(k, count, source):
        def step(cell, total):
            high, low = split(source(cell))
            w_high, w_low = weights[cell, 0:80, :], weights[cell, 160:240, :]
            left = jnp.concatenate([w_high, w_low, w_high], axis=1)
            right = jnp.concatenate([high, high, low], axis=1)
            return total + dot(left, right, NT)

        total = lax.fori_loop(0, CELLS, step, jnp.zeros((80, count), F32), unroll=12)
        wide[:, 0:count] = total
        for s in range(5):
            upper = pltpu.roll(wide[16 * s + 8 : 16 * s + 16, :], 64, 1)
            part[k, s] = jnp.where(lane < 64, wide[16 * s : 16 * s + 8, :], upper)
        start_all(part_copy, k)

    def finish_coef(k):
        arrive_all(part_copy, k)
        total = part[k, 0]
        for s in range(4):
            total = total + part_in[k, s]
        coef[k, 0] = total * energy[...]
        start_all(coef_copy, k)

    def along_z(rows, count, source):
        for x in range(6):
            high, low = split(source(x).reshape(6 * count, 128))
            left = jnp.concatenate([high, low, high], axis=1)
            zn[6 * x : 6 * x + 6, rows] = dot(left, banded[...]).reshape(6, count, 128)

    def projected(k, rows, count):
        arrive_all(coef_copy, k)
        parts = []
        for s in range(5):
            parts += [coef[k, s], pltpu.roll(coef[k, s], 64, 1)]
        stacked = jnp.concatenate(parts, axis=0)
        high = stacked.astype(BF16).astype(F32)
        low = (stacked - high).astype(BF16).astype(F32)
        left = jnp.concatenate([high, low, high], axis=0).T[0:count, :].astype(BF16)

        @pl.loop(0, CELLS, unroll=12)
        def _(cell):
            zn[cell, rows] += dot(left, weights[cell])

    center = -1.5 * stencil_weights[0] - filter_center

    def stencil(phase, c, source, finish):
        for x in range(6):

            def layer(other):
                if other < 0:
                    return halo[phase, c, 0, 6 * (other + 6) : 6 * (other + 7)].astype(F32)
                if other > 5:
                    return halo[phase, c, 1, 6 * (other - 6) : 6 * (other - 5)].astype(F32)
                return source(other)

            here = source(x)
            line_y = jnp.concatenate(
                [
                    halo[phase, c, 2, 6 * x : 6 * x + 6].astype(F32),
                    here,
                    halo[phase, c, 3, 6 * x : 6 * x + 6].astype(F32),
                ],
                axis=0,
            )
            total = zn[6 * x : 6 * x + 6, rows_of(c), :]
            total = total + here * (pot[x][:, None, :] + center)
            for step in range(1, 7):
                weight = -0.5 * stencil_weights[step]
                pair = layer(x - step) + layer(x + step)
                pair = pair + line_y[6 - step : 12 - step] + line_y[6 + step : 12 + step]
                total = total + weight * pair
            finish(x, total)

    everyone = pl.ds(0, ORB)
    partial(0, ORB, lambda cell: y0[cell])
    start_all(halo_copy, 0, 1)
    finish_coef(0)
    start_all(halo_copy, 0, 2)
    start_all(halo_copy, 0, 3)
    along_z(everyone, ORB, lambda x: y0[6 * x : 6 * x + 6])
    loads[2].wait()
    projected(0, everyone, ORB)

    def group_rows(g):
        return pl.ds(pl.multiple_of(g * GROUP, GROUP), GROUP)

    @pl.loop(0, 2)
    def _(g):
        @pl.loop(2 * g, 2 * g + 2)
        def _(c):
            arrive_all(halo_copy, 0, c)

            def finish(x, total):
                value = total * (1.0 / filter_half)
                y1[6 * x : 6 * x + 6, rows_of(c), :] = value
                sent[1, c, 6 * x : 6 * x + 6] = value.astype(BF16)

            stencil(0, c, lambda x: y0[6 * x : 6 * x + 6, rows_of(c), :], finish)

        partial(1 + g, GROUP, lambda cell: y1[cell, group_rows(g), :])
        start_all(halo_copy, 1, g)

    finish_coef(1)
    finish_coef(2)
    start_all(halo_copy, 1, 2)
    start_all(halo_copy, 1, 3)

    def mate_copy(c):
        return remote(own.at[c], mate_in.at[c], s_mate.at[c], r_mate.at[c], mate)

    def far_copy(c):
        start = pl.multiple_of(group * HALF, HALF)
        return remote(
            own.at[c, pl.ds(start, HALF)], far_in.at[c], s_far.at[c], r_far.at[c], far
        )

    def cross_copy(c):
        return remote(far_in.at[c], cross_in.at[c], s_cross.at[c], r_cross.at[c], mate)

    @pl.loop(0, 2)
    def _(g):
        along_z(group_rows(g), GROUP, lambda x: y1[6 * x : 6 * x + 6, group_rows(g), :])
        projected(1 + g, group_rows(g), GROUP)

        @pl.loop(2 * g, 2 * g + 2)
        def _(c):
            arrive_all(halo_copy, 1, c)

            def finish(x, total):
                before = y0[6 * x : 6 * x + 6, rows_of(c), :]
                value = total * (2.0 / filter_half) - before
                out[6 * x : 6 * x + 6, rows_of(c), :] = value
                own[c, 6 * x : 6 * x + 6] = value.astype(BF16)

            stencil(1, c, lambda x: y1[6 * x : 6 * x + 6, rows_of(c), :], finish)
            far_copy(c).start()
            mate_copy(c).start()

    @pl.loop(0, CHUNKS)
    def _(c):
        far_copy(c).wait_recv()
        cross_copy(c).start()

    @pl.loop(0, CHUNKS)
    def _(c):
        mate_copy(c).wait_recv()

    def gather(ref, cell):
        return jnp.concatenate([ref[c, cell] for c in range(CHUNKS)], axis=0)

    def in_order(first, second):
        return jnp.concatenate(
            [jnp.where(core == 0, first, second), jnp.where(core == 0, second, first)], axis=0
        )

    def near_step(cell, total):
        mine = gather(own, cell)
        return total + dot(mine, in_order(mine, gather(mate_in, cell)), NT)

    near_sum = lax.fori_loop(0, CELLS, near_step, jnp.zeros((ORB, 128), F32), unroll=12)

    @pl.loop(0, CHUNKS)
    def _(c):
        cross_copy(c).wait_recv()

    def far_step(cell, totals):
        mine = gather(own, (1 - group) * HALF + cell)
        theirs, others = gather(far_in, cell), gather(cross_in, cell)
        straight = totals[0] + dot(mine, in_order(theirs, others), NT)
        both = jnp.concatenate([theirs, others], axis=0)
        zero = jnp.zeros_like(mine)
        turned = totals[1] + dot(both, in_order(mine, zero), NT)
        return straight, turned

    start = (jnp.zeros((ORB, 128), F32), jnp.zeros((2 * ORB, 128), F32))
    far_sum, turned = lax.fori_loop(0, HALF, far_step, start, unroll=9)

    for q in range(16):
        rows = slice(4 * q, 4 * q + 4)
        sums[q, 0:4] = near_sum[rows]
        sums[q, 4:8] = far_sum[rows]
        sums[q, 8:12] = turned[rows]
        sums[q, 12:16] = turned[ORB + 4 * q : ORB + 4 * q + 4]

    def scat_copy(step):
        other, device = plane_peer(step)
        return remote(
            sums.at[other], scat_in.at[step], s_scat.at[step], r_scat.at[step], device
        )

    def whole_copy(step):
        device = plane_peer(step)[1]
        return remote(
            whole.at[plane], whole.at[plane], s_whole.at[step], r_whole.at[step], device
        )

    def deep_copy(step):
        device = deep_peer(step)[1]
        return remote(deep.at[0], deep_in.at[step], s_deep.at[step], r_deep.at[step], device)

    def turn_copy(side, step):
        device = {**deep_peer(step)[1], **(far, cross)[side]}
        return remote(
            deep.at[1],
            turn_in.at[side, step],
            s_turn.at[side, step],
            r_turn.at[side, step],
            device,
        )

    @pl.loop(1, 16)
    def _(step):
        scat_copy(step).start()

    def add_scat(step, total):
        scat_copy(step).wait_recv()
        return total + scat_in[step]

    mine = lax.fori_loop(1, 16, add_scat, sums[plane])
    deep[0] = mine[0:8]
    deep[1] = mine[8:16]
    for step in range(4):
        for side in range(2):
            turn_copy(side, step).start()
    for step in range(1, 4):
        deep_copy(step).start()
    mine = mine[0:8]
    for step in range(1, 4):
        deep_copy(step).wait_recv()
        mine = mine + deep_in[step]
    turned_in = jnp.zeros((4, 128), F32)
    for step in range(4):
        for side in range(2):
            turn_copy(side, step).wait_recv()
            turned_in = turned_in + turn_in[side, step, 4 * side : 4 * side + 4]
    mine = mine + jnp.concatenate([jnp.zeros((4, 128), F32), turned_in], axis=0)
    whole[plane] = mine * (1.0 / cells_total)

    @pl.loop(1, 16)
    def _(step):
        whole_copy(step).start()

    @pl.loop(1, 16)
    def _(step):
        other = lax.rem(plane + 16 - step, 16)
        remote(
            whole.at[other],
            whole.at[other],
            s_whole.at[step],
            r_whole.at[step],
            plane_peer(step)[1],
        ).wait_recv()

    for q in range(16):
        near_rows, far_rows = whole[q, 0:4], whole[q, 4:8]
        gram[4 * q : 4 * q + 4, 0:128] = jnp.where(group == 0, near_rows, far_rows)
        gram[4 * q : 4 * q + 4, 128:256] = jnp.where(group == 0, far_rows, near_rows)

    sent_all(msg_copy)
    for phase in range(2):

        @pl.loop(0, CHUNKS)
        def _(c, phase=phase):
            sent_all(halo_copy, phase, c)

    @pl.loop(0, 3)
    def _(k):
        sent_all(part_copy, k)
        sent_all(coef_copy, k)

    @pl.loop(0, CHUNKS)
    def _(c):
        mate_copy(c).wait_send()
        far_copy(c).wait_send()
        cross_copy(c).wait_send()

    @pl.loop(1, 16)
    def _(step):
        scat_copy(step).wait_send()
        whole_copy(step).wait_send()

    for step in range(4):
        for side in range(2):
            turn_copy(side, step).wait_send()
    for step in range(1, 4):
        deep_copy(step).wait_send()


def local(orbitals, potential, projectors, energies, centers):
    y0 = orbitals.transpose(1, 2, 0, 3).reshape(CELLS, ORB, 128)
    proj = projectors.transpose(0, 2, 1, 3)
    cells_total = CELLS * 128 * lax.axis_size("sx") * lax.axis_size("sy")
    vmem = pl.BlockSpec(memory_space=pltpu.VMEM)
    anywhere = pl.BlockSpec(memory_space=pl.ANY)
    smem = pl.BlockSpec(memory_space=pltpu.SMEM)
    dma = pltpu.SemaphoreType.DMA
    chunk = (CHUNKS, CELLS, ROWS, 128)
    half = (CHUNKS, HALF, ROWS, 128)
    out, gram = pl.pallas_call(
        functools.partial(kernel, cells_total),
        out_shape=(
            jax.ShapeDtypeStruct((CELLS, ORB, 128), F32),
            jax.ShapeDtypeStruct((ORB, 256), F32),
        ),
        in_specs=[anywhere, anywhere, anywhere, smem, smem],
        out_specs=(vmem, vmem),
        scratch_shapes=[
            pltpu.VMEM((CELLS, ORB, 128), F32),
            pltpu.VMEM((6, 6, 128), F32),
            pltpu.VMEM((4, 5, 4, 128), F32),
            pltpu.VMEM((CELLS, ORB, 128), F32),
            pltpu.VMEM((CELLS, ORB, 128), F32),
            pltpu.VMEM((5, MSG_ROWS, 128), F32),
            pltpu.VMEM((CELLS, 240, 128), BF16),
            pltpu.VMEM((384, 128), BF16),
            pltpu.VMEM((2,) + chunk, BF16),
            pltpu.VMEM((2, CHUNKS, 4, CELLS, ROWS, 128), BF16),
            pltpu.VMEM((3, 5, 8, 128), F32),
            pltpu.VMEM((3, 4, 8, 128), F32),
            pltpu.VMEM((3, 5, 8, 128), F32),
            pltpu.VMEM((8, 128), F32),
            pltpu.VMEM((80, 128), F32),
            pltpu.VMEM(chunk, BF16),
            pltpu.VMEM(chunk, BF16),
            pltpu.VMEM(half, BF16),
            pltpu.VMEM(half, BF16),
            pltpu.VMEM((16, 16, 128), F32),
            pltpu.VMEM((16, 16, 128), F32),
            pltpu.VMEM((2, 8, 128), F32),
            pltpu.VMEM((4, 8, 128), F32),
            pltpu.VMEM((2, 4, 8, 128), F32),
            pltpu.VMEM((16, 8, 128), F32),
            dma((3,)),
            dma((4,)),
            dma((4,)),
            dma((2, CHUNKS, 4)),
            dma((2, CHUNKS, 4)),
            dma((3, 4)),
            dma((3, 4)),
            dma((3, 4)),
            dma((3, 4)),
            dma((CHUNKS,)),
            dma((CHUNKS,)),
            dma((CHUNKS,)),
            dma((CHUNKS,)),
            dma((CHUNKS,)),
            dma((CHUNKS,)),
            dma((16,)),
            dma((16,)),
            dma((4,)),
            dma((4,)),
            dma((2, 4)),
            dma((2, 4)),
            dma((16,)),
            dma((16,)),
        ],
        compiler_params=pltpu.CompilerParams(
            collective_id=0, has_side_effects=True, vmem_limit_bytes=48 * 1024 * 1024
        ),
        name="filter_and_gram",
    )(y0, potential, proj, energies, centers.T)
    filtered = out.reshape(6, 6, ORB, 128).transpose(2, 0, 1, 3)
    return filtered, gram


def solution(mesh):
    in_specs = (
        P("band", "sx", "sy", None),
        P("sx", "sy", None),
        P(("sx", "sy"), None, None, None),
        P(("sx", "sy"), None),
        P(("sx", "sy"), None),
    )
    out_specs = (P("band", "sx", "sy", None), P("band", None))
    return jax.shard_map(local, mesh=mesh, in_specs=in_specs, out_specs=out_specs, check_vma=False)
```

time: 136 us -> 107 us (0.79)
  Pallas kernels: 129 us -> 99.9 us
    pallas_call x1, Pallas kernels: 129 us -> 99.9 us  [local(): pl.pallas_call(functools.partial(kernel, cells_total), out_shape=(jax.Sha...]
    unnamed x11 -> x12, local copies, waits for them, and re-layouts: 5.88 us -> 5.78 us
where the time goes in v2:
time: 107 us; the launch traced here: 106 us
  Pallas kernels  99.9 us (93%)
  local copies, waits for them, and re-layouts  5.78 us (5%)
    pallas_call x1, Pallas kernels, local(): pl.pallas_call(functools.partial(kernel, cells_total), out_shape=(jax.Sha...  99.9 us
    unnamed x12, local copies, waits for them, and re-layouts  5.78 us

profile of v2, /device:TPU:1, one launch (start us, length us, event | category | flops | bytes accessed | tf_op | source)
XLA Modules:
  0.0 106.3 jit_solution(6712957718015652675)
XLA Ops:
  0.6 0.0 copy-start
  0.6 1.3 %copy-done = f32[64,6,6,128]{3,0,2,1:T(8,128)S(1)} copy-done((f32[64,6,6,128]{3,0,2,1:T(8,128)S(1)}, f32[64,6,6,128]{3,0,2,1:T(8,128)}, u32[]{:S(2)}) %copy-start) | copy-done | bytes 1179672
  1.9 0.0 copy-start.1
  1.9 0.8 copy-done.1
  2.7 0.0 copy-start.2
  2.7 0.7 copy-done.2
  3.4 0.0 copy-start.3
  3.4 0.7 copy-done.3
  4.1 0.0 copy-start.4
  4.1 0.7 copy-done.4
  4.8 99.9 %filter_and_gram.1 = (f32[36,64,128]{2,1,0:T(8,128)S(1)}, f32[64,256]{1,0:T(8,128)S(1)}) custom-call(f32[36,64,128]{2,1,0:T(8,128)S(1)} %bitcast.8, f32[6,6,128]{2,1,0:T(8,128)S(1)} %copy-done.2, f32[4,5,4,128]{3,2,1,0:T(4,128)S(1)} %bitcast.10, f32[4,4]{1,0:T(4,128)S(1)} %copy-done.3, s32[2,4]{1,0:T(2,128)S(1)} %bitcast.11), custom_call_target="tpu_custom_call" | custom-call | tf_op jit(solution)/shard_map/filter_and_gram/pallas_call | solution.py:606
  104.7 1.0 copy.9
  105.7 0.6 copy.10
Async XLA Ops:
  0.6 1.3 %copy-start = (f32[64,6,6,128]{3,0,2,1:T(8,128)S(1)}, f32[64,6,6,128]{3,0,2,1:T(8,128)}, u32[]{:S(2)}) copy-start(f32[64,6,6,128]{3,0,2,1:T(8,128)} %param.5) | copy-start | bytes 3538948
  1.9 0.8 copy-start.1
  2.7 0.7 copy-start.2
  3.4 0.7 copy-start.3
  4.1 0.7 copy-start.4

commit v3 on v2

--- a/solution.py
+++ b/solution.py
@@ -29,7 +29,7 @@
 CELLS = 36
 HALF = CELLS // 2
 PAIRS = 20
-MSG_ROWS = 4 * PAIRS + 8
+NEAR_ROWS = 24
 GROUP = ORB // 2
 NT = (((1,), (1,)), ((), ()))
 NN = (((1,), (0,)), ((), ()))
@@ -51,14 +51,16 @@
     proj_hbm,
     energies,
     centers,
+    out_hbm,
+    gram,
     out,
-    gram,
     y0,
     pot,
     proj,
     y1,
     zn,
     msg,
+    msg_in,
     weights,
     banded,
     sent,
@@ -79,6 +81,7 @@
     turn_in,
     whole,
     s_load,
+    s_store,
     s_msg,
     r_msg,
     s_halo,
@@ -162,34 +165,39 @@
         greet({**device, **cross})
 
     lane = lax.broadcasted_iota(jnp.int32, (8, 128), 1)
+    line = lax.broadcasted_iota(jnp.int32, (8, 128), 0)
     atom = lane // 5
     tile = lane - atom * 5
     shift_x = jnp.where(tile == 1, -1, jnp.where(tile == 2, 1, 0))
     shift_y = jnp.where(tile == 3, -1, jnp.where(tile == 4, 1, 0))
-    cell_x = jnp.full((8, 128), -1000, jnp.int32)
-    cell_y = jnp.full((8, 128), -1000, jnp.int32)
+    nowhere = jnp.full((8, 128), -1000, jnp.int32)
+    cell_x, cell_y, near_x, near_y = nowhere, nowhere, nowhere, nowhere
     for a in range(4):
         cell_x = jnp.where(atom == a, centers[0, a], cell_x)
         cell_y = jnp.where(atom == a, centers[1, a], cell_y)
-    line = lax.broadcasted_iota(jnp.int32, (8, 128), 0)
-    cells = jnp.where(line == 0, cell_x + shift_x, cell_y + shift_y)
-    msg[0, 4 * PAIRS : MSG_ROWS, :] = cells.astype(F32)
+        near_x = jnp.where(lane == a, centers[0, a], near_x)
+        near_y = jnp.where(lane == a, centers[1, a], near_y)
+    own_cells = jnp.where(line == 0, cell_x + shift_x, cell_y + shift_y).astype(F32)
     loads[0].wait()
-    for p in range(4):
-        for a in range(4):
-            start = p * PAIRS + 5 * a
-            msg[0, start : start + 5, :] = proj[a, :, p, :]
-
+    for s, (step_x, step_y) in enumerate(((-1, 0), (1, 0), (0, -1), (0, 1))):
+        shifted = jnp.where(line == 0, near_x + step_x, near_y + step_y)
+        msg[s, 16:24, :] = shifted.astype(F32)
+        for p in range(4):
+            msg[s, 4 * p : 4 * p + 4, :] = proj[:, s + 1, p, :]
     for s in range(4):
 
         @pl.when(jnp.logical_not(has[s]))
         def _(s=s):
-            msg[1 + s] = jnp.zeros((MSG_ROWS, 128), F32)
-            msg[1 + s, 4 * PAIRS : MSG_ROWS] = jnp.full((8, 128), -1000.0, F32)
+            msg_in[s, 0:16] = jnp.zeros((16, 128), F32)
+            msg_in[s, 16:24] = jnp.full((8, 128), -1000.0, F32)
             for phase in range(2):
-                for c in range(CHUNKS):
+
+                @pl.loop(0, CHUNKS)
+                def _(c, phase=phase):
                     halo[phase, c, s] = jnp.zeros((CELLS, ROWS, 128), BF16)
-            for k in range(3):
+
+            @pl.loop(0, 3)
+            def _(k):
                 part_in[k, s] = jnp.zeros((8, 128), F32)
                 coef[k, 1 + s] = jnp.zeros((8, 128), F32)
 
@@ -219,14 +227,15 @@
         return pl.ds(pl.multiple_of(c * ROWS, ROWS), ROWS)
 
     loads[1].wait()
-    for c in range(CHUNKS):
-        for x in range(6):
-            sent[0, c, 6 * x : 6 * x + 6] = y0[6 * x : 6 * x + 6, rows_of(c), :].astype(BF16)
+    @pl.loop(0, CHUNKS)
+    def _(c):
+        sent[0, c] = y0[:, rows_of(c), :].astype(BF16)
+
 
     pl.semaphore_wait(barrier, 7 + 15 + 9)
 
     def msg_copy(s):
-        return remote(msg.at[0], msg.at[1 + (s ^ 1)], s_msg.at[s], r_msg.at[s ^ 1], near[s])
+        return remote(msg.at[s], msg_in.at[s ^ 1], s_msg.at[s], r_msg.at[s ^ 1], near[s])
 
     def halo_copy(phase, c, s):
         return remote(
@@ -273,21 +282,24 @@
 
     arrive_all(msg_copy)
     first_x, first_y = (ix * 6).astype(F32), (iy * 6).astype(F32)
-    key = jnp.full((1, 128), -1000.0, F32)
-    wide_atom = atom.astype(F32)
-    for s in range(5):
-        coords = msg[s, 4 * PAIRS : MSG_ROWS, :]
+    def placed_rows(coords, which, count):
         local_x, local_y = coords[0:1] - first_x, coords[1:2] - first_y
         inside = (local_x >= 0) & (local_x < 6) & (local_y >= 0) & (local_y < 6)
-        inside = inside & (lane[0:1] < PAIRS)
-        place = (local_x * 6 + local_y) * 80 + (16.0 * s + wide_atom[0:1])
-        place = jnp.broadcast_to(jnp.where(inside, place, -1000.0), (8, 128))
-        moved = pltpu.roll(place, PAIRS * s, 1)[0:1] if s else place[0:1]
-        mine = (lane[0:1] >= PAIRS * s) & (lane[0:1] < PAIRS * (s + 1))
-        key = jnp.where(mine, moved, key)
+        inside = inside & (lane[0:1] < count)
+        place = jnp.where(inside, (local_x * 6 + local_y) * 80 + which, -1000.0)
+        return jnp.broadcast_to(place, (8, 128))
+
+    key = placed_rows(own_cells, atom[0:1].astype(F32), PAIRS)
+    for s in range(4):
+        start = PAIRS + 4 * s
+        which = lane[0:1].astype(F32) + 16.0 * (s + 1)
+        moved = pltpu.roll(placed_rows(msg_in[s, 16:24, :], which, 4), start, 1)
+        key = jnp.where((lane >= start) & (lane < start + 4), moved, key)
+    key = jnp.where(lane < 64, key, pltpu.roll(key, 64, 1) + 4.0)[0:1]
     tables = []
     for p in range(4):
-        stacked = [msg[s, p * PAIRS : (p + 1) * PAIRS, :] for s in range(5)]
+        stacked = [proj[a, :, p, :] for a in range(4)]
+        stacked += [msg_in[s, 4 * p : 4 * p + 4, :] for s in range(4)]
         table = jnp.concatenate(stacked + [jnp.zeros((28, 128), F32)], axis=0)
         tables.append(jnp.concatenate(split(table), axis=1))
     table = jnp.concatenate(tables, axis=0)
@@ -296,9 +308,7 @@
     def _(block):
         row = lax.broadcasted_iota(jnp.int32, (320, 128), 0) + block * 320
         row = row.astype(F32)
-        masks = [
-            jnp.where(row == key + 4.0 * p, 1.0, 0.0).astype(BF16) for p in range(4)
-        ]
+        masks = [jnp.where(row == key + 8.0 * p, 1.0, 0.0).astype(BF16) for p in range(2)]
         placed = dot(jnp.concatenate(masks, axis=1), table)
         placed = placed.reshape(4, 80, 256).astype(BF16)
         weights[pl.ds(block * 4, 4), 0:80, :] = placed[:, :, :128]
@@ -412,6 +422,11 @@
     start_all(halo_copy, 1, 2)
     start_all(halo_copy, 1, 3)
 
+    def store_copy(c):
+        return pltpu.make_async_copy(
+            out.at[:, rows_of(c), :], out_hbm.at[:, rows_of(c), :], s_store.at[c]
+        )
+
     def mate_copy(c):
         return remote(own.at[c], mate_in.at[c], s_mate.at[c], r_mate.at[c], mate)
 
@@ -442,29 +457,31 @@
             stencil(1, c, lambda x: y1[6 * x : 6 * x + 6, rows_of(c), :], finish)
             far_copy(c).start()
             mate_copy(c).start()
+            store_copy(c).start()
+
+    @pl.loop(0, CHUNKS)
+    def _(c):
+        mate_copy(c).wait_recv()
+
+    def gather(ref, cell):
+        return jnp.concatenate([ref[c, cell] for c in range(CHUNKS)], axis=0)
+
+    def in_order(first, second):
+        return jnp.concatenate(
+            [jnp.where(core == 0, first, second), jnp.where(core == 0, second, first)], axis=0
+        )
+
+    def near_step(cell, total):
+        mine = gather(own, cell)
+        return total + dot(mine, in_order(mine, gather(mate_in, cell)), NT)
+
+    near_sum = lax.fori_loop(0, CELLS, near_step, jnp.zeros((ORB, 128), F32), unroll=12)
+    sums[:, 0:4] = near_sum.reshape(16, 4, 128)
 
     @pl.loop(0, CHUNKS)
     def _(c):
         far_copy(c).wait_recv()
         cross_copy(c).start()
-
-    @pl.loop(0, CHUNKS)
-    def _(c):
-        mate_copy(c).wait_recv()
-
-    def gather(ref, cell):
-        return jnp.concatenate([ref[c, cell] for c in range(CHUNKS)], axis=0)
-
-    def in_order(first, second):
-        return jnp.concatenate(
-            [jnp.where(core == 0, first, second), jnp.where(core == 0, second, first)], axis=0
-        )
-
-    def near_step(cell, total):
-        mine = gather(own, cell)
-        return total + dot(mine, in_order(mine, gather(mate_in, cell)), NT)
-
-    near_sum = lax.fori_loop(0, CELLS, near_step, jnp.zeros((ORB, 128), F32), unroll=12)
 
     @pl.loop(0, CHUNKS)
     def _(c):
@@ -482,12 +499,9 @@
     start = (jnp.zeros((ORB, 128), F32), jnp.zeros((2 * ORB, 128), F32))
     far_sum, turned = lax.fori_loop(0, HALF, far_step, start, unroll=9)
 
-    for q in range(16):
-        rows = slice(4 * q, 4 * q + 4)
-        sums[q, 0:4] = near_sum[rows]
-        sums[q, 4:8] = far_sum[rows]
-        sums[q, 8:12] = turned[rows]
-        sums[q, 12:16] = turned[ORB + 4 * q : ORB + 4 * q + 4]
+    sums[:, 4:8] = far_sum.reshape(16, 4, 128)
+    sums[:, 8:12] = turned[:ORB].reshape(16, 4, 128)
+    sums[:, 12:16] = turned[ORB:].reshape(16, 4, 128)
 
     def scat_copy(step):
         other, device = plane_peer(step)
@@ -558,10 +572,10 @@
             plane_peer(step)[1],
         ).wait_recv()
 
-    for q in range(16):
-        near_rows, far_rows = whole[q, 0:4], whole[q, 4:8]
-        gram[4 * q : 4 * q + 4, 0:128] = jnp.where(group == 0, near_rows, far_rows)
-        gram[4 * q : 4 * q + 4, 128:256] = jnp.where(group == 0, far_rows, near_rows)
+    near_all = whole[:, 0:4].reshape(ORB, 128)
+    far_all = whole[:, 4:8].reshape(ORB, 128)
+    gram[:, 0:128] = jnp.where(group == 0, near_all, far_all)
+    gram[:, 128:256] = jnp.where(group == 0, far_all, near_all)
 
     sent_all(msg_copy)
     for phase in range(2):
@@ -577,6 +591,7 @@
 
     @pl.loop(0, CHUNKS)
     def _(c):
+        store_copy(c).wait()
         mate_copy(c).wait_send()
         far_copy(c).wait_send()
         cross_copy(c).wait_send()
@@ -610,14 +625,16 @@
             jax.ShapeDtypeStruct((ORB, 256), F32),
         ),
         in_specs=[anywhere, anywhere, anywhere, smem, smem],
-        out_specs=(vmem, vmem),
+        out_specs=(anywhere, vmem),
         scratch_shapes=[
+            pltpu.VMEM((CELLS, ORB, 128), F32),
             pltpu.VMEM((CELLS, ORB, 128), F32),
             pltpu.VMEM((6, 6, 128), F32),
             pltpu.VMEM((4, 5, 4, 128), F32),
             pltpu.VMEM((CELLS, ORB, 128), F32),
             pltpu.VMEM((CELLS, ORB, 128), F32),
-            pltpu.VMEM((5, MSG_ROWS, 128), F32),
+            pltpu.VMEM((4, NEAR_ROWS, 128), F32),
+            pltpu.VMEM((4, NEAR_ROWS, 128), F32),
             pltpu.VMEM((CELLS, 240, 128), BF16),
             pltpu.VMEM((384, 128), BF16),
             pltpu.VMEM((2,) + chunk, BF16),
@@ -638,6 +655,7 @@
             pltpu.VMEM((2, 4, 8, 128), F32),
             pltpu.VMEM((16, 8, 128), F32),
             dma((3,)),
+            dma((CHUNKS,)),
             dma((4,)),
             dma((4,)),
             dma((2, CHUNKS, 4)),
@@ -662,7 +680,7 @@
             dma((16,)),
         ],
         compiler_params=pltpu.CompilerParams(
-            collective_id=0, has_side_effects=True, vmem_limit_bytes=48 * 1024 * 1024
+            collective_id=0, has_side_effects=True, vmem_limit_bytes=60 * 1024 * 1024
         ),
         name="filter_and_gram",
     )(y0, potential, proj, energies, centers.T)

time: 107 us -> 102 us (0.953)
  local copies, waits for them, and re-layouts: 5.78 us -> 3.08 us
  Pallas kernels: 99.9 us -> 98.6 us
    unnamed x12 -> x4, local copies, waits for them, and re-layouts: 5.78 us -> 3.08 us
    pallas_call x1, Pallas kernels: 99.9 us -> 98.6 us  [local(): pl.pallas_call(functools.partial(kernel, cells_total), out_shape=(jax.Sha...]
where the time goes in v3:
time: 102 us
  Pallas kernels  98.6 us (97%)
  local copies, waits for them, and re-layouts  3.08 us (3%)
    pallas_call x1, Pallas kernels, local(): pl.pallas_call(functools.partial(kernel, cells_total), out_shape=(jax.Sha...  98.6 us
    unnamed x4, local copies, waits for them, and re-layouts  3.08 us

profile of v3, /device:TPU:1, one launch (start us, length us, event | category | flops | bytes accessed | tf_op | source)
XLA Modules:
  0.0 102.3 jit_solution(16531512277196147730)
XLA Ops:
  0.6 98.6 %filter_and_gram.1 = (f32[36,64,128]{2,1,0:T(8,128)}, f32[64,256]{1,0:T(8,128)}) custom-call(f32[36,64,128]{2,1,0:T(8,128)} %bitcast.8, f32[6,6,128]{2,1,0:T(8,128)} %pot_hbm.1, f32[4,5,4,128]{3,2,1,0:T(4,128)} %bitcast.10, f32[4,4]{1,0:T(4,128)} %energies.1, s32[2,4]{1,0:T(2,128)} %bitcast.11), custom_call_target="tpu_custom_call" | custom-call | tf_op jit(solution)/shard_map/filter_and_gram/pallas_call | solution.py:621
  99.2 0.0 copy-start
  99.2 2.4 %copy.9 = f32[64,6,6,128]{3,0,2,1:T(8,128)} copy(f32[64,6,6,128]{3,0,2,1:T(8,128)} %bitcast.9) | data formatting | bytes 2359296
  101.6 0.0 copy-done
  101.7 0.6 copy.10
Async XLA Ops:
  99.2 2.5 %copy-start = (f32[64,256]{1,0:T(8,128)S(1)}, f32[64,256]{1,0:T(8,128)}, u32[]{:S(2)}) copy-start(f32[64,256]{1,0:T(8,128)} %get-tuple-element.9) | copy-start | bytes 196612

commit v4 on v3

--- a/solution.py
+++ b/solution.py
@@ -257,7 +257,7 @@
         )
 
     def start_all(copy, *index):
-        for s in range(4):
+        for s in (2, 3, 0, 1):
 
             @pl.when(has[s])
             def _(s=s):
@@ -606,6 +606,26 @@
             turn_copy(side, step).wait_send()
     for step in range(1, 4):
         deep_copy(step).wait_send()
+
+
+def hand_on(out_from, gram_from, out_to, gram_to, out_here, gram_here, load_sem, store_sem):
+    loads = [pltpu.make_async_copy(gram_from, gram_here, load_sem.at[CHUNKS])]
+    stores = [pltpu.make_async_copy(gram_here, gram_to, store_sem.at[CHUNKS])]
+    for c in range(CHUNKS):
+        part = pl.ds(c * (CELLS // CHUNKS), CELLS // CHUNKS)
+        loads.append(
+            pltpu.make_async_copy(out_from.at[part], out_here.at[part], load_sem.at[c])
+        )
+        stores.append(
+            pltpu.make_async_copy(out_here.at[part], out_to.at[part], store_sem.at[c])
+        )
+    for load in loads:
+        load.start()
+    for load, store in zip(loads, stores):
+        load.wait()
+        store.start()
+    for store in stores:
+        store.wait()
 
 
 def local(orbitals, potential, projectors, energies, centers):
@@ -684,6 +704,23 @@
         ),
         name="filter_and_gram",
     )(y0, potential, proj, energies, centers.T)
+    out, gram = pl.pallas_call(
+        hand_on,
+        out_shape=(
+            jax.ShapeDtypeStruct((CELLS, ORB, 128), F32),
+            jax.ShapeDtypeStruct((ORB, 256), F32),
+        ),
+        in_specs=[anywhere, anywhere],
+        out_specs=(anywhere, anywhere),
+        scratch_shapes=[
+            pltpu.VMEM((CELLS, ORB, 128), F32),
+            pltpu.VMEM((ORB, 256), F32),
+            dma((CHUNKS + 1,)),
+            dma((CHUNKS + 1,)),
+        ],
+        compiler_params=pltpu.CompilerParams(vmem_limit_bytes=60 * 1024 * 1024),
+        name="hand_on",
+    )(out, gram)
     filtered = out.reshape(6, 6, ORB, 128).transpose(2, 0, 1, 3)
     return filtered, gram
 

time: 102 us -> 101 us (level)
  local copies, waits for them, and re-layouts: 3.08 us -> 0 us
  Pallas kernels: 98.6 us -> 101 us
    unnamed x4 -> x0, local copies, waits for them, and re-layouts: 3.08 us -> none
    pallas_call x0 -> x1, Pallas kernels: none -> 2.09 us  [local(): pl.pallas_call(hand_on, out_shape=(jax.ShapeDtypeStruct((CELLS, ORB, 128)...]
where the time goes in v4:
time: 101 us
  Pallas kernels  101 us (100%)
    pallas_call x1, Pallas kernels, local(): pl.pallas_call(functools.partial(kernel, cells_total), out_shape=(jax.Sha...  98.6 us
    pallas_call x1, Pallas kernels, local(): pl.pallas_call(hand_on, out_shape=(jax.ShapeDtypeStruct((CELLS, ORB, 128)...  2.09 us

profile of v4, /device:TPU:1, one launch (start us, length us, event | category | flops | bytes accessed | tf_op | source)
XLA Modules:
  0.0 101.3 jit_solution(17786910495404631106)
XLA Ops:
  0.6 98.6 %filter_and_gram.1 = (f32[36,64,128]{2,1,0:T(8,128)}, f32[64,256]{1,0:T(8,128)}) custom-call(f32[36,64,128]{2,1,0:T(8,128)} %bitcast.8, f32[6,6,128]{2,1,0:T(8,128)} %pot_hbm.1, f32[4,5,4,128]{3,2,1,0:T(4,128)} %bitcast.9, f32[4,4]{1,0:T(4,128)} %energies.1, s32[2,4]{1,0:T(2,128)} %bitcast.10), custom_call_target="tpu_custom_call" | custom-call | tf_op jit(solution)/shard_map/filter_and_gram/pallas_call | solution.py:641
  99.2 2.1 %hand_on.1 = (f32[36,64,128]{2,1,0:T(8,128)}, f32[64,256]{1,0:T(8,128)}) custom-call(f32[36,64,128]{2,1,0:T(8,128)} %get-tuple-element.6.out_from, f32[64,256]{1,0:T(8,128)} %get-tuple-element.7.gram_from), custom_call_target="tpu_custom_call" | custom-call | tf_op jit(solution)/shard_map/hand_on/pallas_call | solution.py:707

commit v5 on v4

--- a/solution.py
+++ b/solution.py
@@ -256,8 +256,8 @@
             coef.at[k, 0], coef.at[k, 1 + (s ^ 1)], s_coef.at[k, s], r_coef.at[k, s ^ 1], near[s]
         )
 
-    def start_all(copy, *index):
-        for s in (2, 3, 0, 1):
+    def start_all(copy, *index, sides=(2, 3, 0, 1)):
+        for s in sides:
 
             @pl.when(has[s])
             def _(s=s):
@@ -277,8 +277,9 @@
             def _(s=s):
                 copy(*index, s).wait_send()
 
-    start_all(msg_copy)
-    start_all(halo_copy, 0, 0)
+    for sides in ((2, 3), (0, 1)):
+        start_all(msg_copy, sides=sides)
+        start_all(halo_copy, 0, 0, sides=sides)
 
     arrive_all(msg_copy)
     first_x, first_y = (ix * 6).astype(F32), (iy * 6).astype(F32)

time: 101 us -> 101 us (level)
  no operation moved by 1% of the time
where the time goes in v5:
time: 101 us
  Pallas kernels  101 us (100%)
    pallas_call x1, Pallas kernels, local(): pl.pallas_call(functools.partial(kernel, cells_total), out_shape=(jax.Sha...  98.6 us
    pallas_call x1, Pallas kernels, local(): pl.pallas_call(hand_on, out_shape=(jax.ShapeDtypeStruct((CELLS, ORB, 128)...  2.09 us

profile of v5, /device:TPU:1, one launch (start us, length us, event | category | flops | bytes accessed | tf_op | source)
XLA Modules:
  0.0 101.3 jit_solution(16673744747799696168)
XLA Ops:
  0.6 98.6 %filter_and_gram.1 = (f32[36,64,128]{2,1,0:T(8,128)}, f32[64,256]{1,0:T(8,128)}) custom-call(f32[36,64,128]{2,1,0:T(8,128)} %bitcast.8, f32[6,6,128]{2,1,0:T(8,128)} %pot_hbm.1, f32[4,5,4,128]{3,2,1,0:T(4,128)} %bitcast.9, f32[4,4]{1,0:T(4,128)} %energies.1, s32[2,4]{1,0:T(2,128)} %bitcast.10), custom_call_target="tpu_custom_call" | custom-call | tf_op jit(solution)/shard_map/filter_and_gram/pallas_call | solution.py:642
  99.2 2.1 %hand_on.1 = (f32[36,64,128]{2,1,0:T(8,128)}, f32[64,256]{1,0:T(8,128)}) custom-call(f32[36,64,128]{2,1,0:T(8,128)} %get-tuple-element.6.out_from, f32[64,256]{1,0:T(8,128)} %get-tuple-element.7.gram_from), custom_call_target="tpu_custom_call" | custom-call | tf_op jit(solution)/shard_map/hand_on/pallas_call | solution.py:708
